TPU v7x, 128 devices: a whole 4x4x4 slice. The times are simulated.
128 devices in a mesh: bin: 8 (over x, core), freq: 16 (over z, y).
Axes of the slice: x: 4, y: 4, z: 4, core: 2. Of those that a mesh axis runs over, the one named last changes fastest.
Arguments:
- traces: bfloat16 [131072, 2048], P(('bin', 'freq')), may hold values from -6 to 6
- rcv_index: int32 [131072], P(('bin', 'freq')), may hold values from 0 to 511, as said below
- src_index: int32 [131072], P(('bin', 'freq')), may hold values from 0 to 511, as said below
- wave_filter: float32 [2, 256], P(None, 'freq'), may hold values from -8 to 8
Outputs:
- multiples: bfloat16 [2, 256, 512, 512], P(None, 'freq', 'bin')
Inputs may be any that keep to these rules, and one draw needn't show every extreme that they name: rcv_index and src_index name each (receiver, source) cell at most once. Group the receiver bins in runs of 4 consecutive ones: every device holds the same number of traces of a given run, at most 16, and in some run exactly 16 on every device. `src_index`: source bin of the trace, paired with rcv_index as above.
All inputs are finite; a program needn't handle non-finite values.
Results may differ from a plain program's by a relative error of at most 0.0058.
Values may be sent and summed in bfloat16 or wider, within the bound.
A program may use at most 128 MiB of HBM per device.

v0:
```python
import functools
import math

import jax
import jax.numpy as jnp
import numpy as np
from jax import lax
from jax.experimental import pallas as pl
from jax.experimental.pallas import tpu as pltpu
from jax.sharding import PartitionSpec as P
import ml_dtypes

ORDER = 512
NT = 2048
NF = 256
DEV = 128
TR = 1024
F32 = jnp.float32
BF16 = jnp.bfloat16
I32 = jnp.int32
LIMIT = 56 * 1024 * 1024


def dft_tables():
    comp = np.arange(4)[:, None]
    dev = np.arange(DEV)[None, :]
    freq = ((dev % 16) * 16 + (dev // 16) * 2 + comp // 2).reshape(-1)
    part = np.broadcast_to(comp % 2, (4, DEV)).reshape(-1)
    phase = (np.arange(NT)[:, None] * freq[None, :]) % NT
    angle = 2.0 * np.pi / NT * phase
    table = np.where(part[None, :] == 0, np.cos(angle), -np.sin(angle)) / math.sqrt(NT)
    high = table.astype(ml_dtypes.bfloat16)
    low = (table - high.astype(np.float64)).astype(ml_dtypes.bfloat16)
    return high, low


def index_kernel(rcv_ref, src_ref, order_ref, slots_ref, count_ref, start_ref):
    rcv = rcv_ref[...]
    src = src_ref[...]
    lane = lax.broadcasted_iota(I32, (TR, DEV), 1)
    member = (rcv // 4 == lane).astype(F32)
    row_i = lax.broadcasted_iota(I32, (DEV, DEV), 0)
    col_i = lax.broadcasted_iota(I32, (DEV, DEV), 1)
    lower = (col_i < row_i).astype(BF16)
    upper = (row_i < col_i).astype(BF16)
    carry = jnp.zeros((1, DEV), F32)
    ranks = []
    for blk in range(TR // DEV):
        m = member[blk * DEV : (blk + 1) * DEV]
        ranks.append(jnp.dot(lower, m.astype(BF16), preferred_element_type=F32) + carry)
        carry = carry + jnp.sum(m, axis=0, keepdims=True)
    rank_all = jnp.concatenate(ranks, axis=0)
    counts8 = jnp.broadcast_to(carry, (8, DEV))
    start = jnp.dot(counts8.astype(BF16), upper, preferred_element_type=F32)
    rank = jnp.sum(member * rank_all, axis=1, keepdims=True)
    first = jnp.sum(member * start[0:1], axis=1, keepdims=True)
    order_ref[...] = (rank + first).astype(I32)
    count_ref[...] = counts8.astype(I32)
    start_ref[...] = start.astype(I32)
    high = ((src // 128) * 4 + rcv % 4 + 1).astype(F32)
    low = (src % 128).astype(F32)
    value = jnp.where(lane < 16, high, jnp.where(lane < 32, low, 0.0))
    value = jnp.where(rank.astype(I32) == lane % 16, value, 0.0)
    slots_ref[...] = lax.dot_general(
        member.astype(BF16), value.astype(BF16), (((0,), (0,)), ((), ())), preferred_element_type=F32
    ).astype(BF16)


def inverse_kernel(slots_ref, code_ref):
    slots = slots_ref[...].astype(F32).T
    sub16 = lax.broadcasted_iota(I32, (16, DEV), 0).astype(F32)
    sub128 = lax.broadcasted_iota(I32, (DEV, DEV), 0).astype(F32)
    dev = lax.broadcasted_iota(I32, (16, DEV), 1).astype(F32)
    acc = jnp.zeros((32, DEV), F32)
    for j in range(16):
        hit = slots[j : j + 1] == sub16 + 1.0
        left = jnp.concatenate([jnp.where(hit, float(j + 1), 0.0), jnp.where(hit, dev, 0.0)], axis=0)
        right = (slots[16 + j : 17 + j] == sub128).astype(F32)
        acc = acc + lax.dot_general(
            left.astype(BF16), right.astype(BF16), (((1,), (1,)), ((), ())), preferred_element_type=F32
        )
    slot = acc[:16]
    code = jnp.where(slot > 0.5, (slot - 1.0) * 128.0 + acc[16:], 4096.0)
    code_ref[...] = code.astype(I32).astype(jnp.int16)


def spectrum_kernel(steps, traces_ref, high_ref, low_ref, order_ref, out_ref, acc_ref):
    step = pl.program_id(0)

    @pl.when(step == 0)
    def _():
        acc_ref[...] = jnp.zeros_like(acc_ref)

    x = traces_ref[...]
    acc_ref[...] += jnp.dot(x, high_ref[...], preferred_element_type=F32) + jnp.dot(
        x, low_ref[...], preferred_element_type=F32
    )

    @pl.when(step == steps - 1)
    def _():
        pick = (order_ref[...] == lax.broadcasted_iota(I32, (TR, TR), 1)).astype(F32).astype(BF16)
        for comp in range(4):
            spec = acc_ref[:, comp * DEV : (comp + 1) * DEV].astype(BF16)
            out_ref[:, comp * TR : (comp + 1) * TR] = lax.dot_general(
                spec, pick, (((0,), (0,)), ((), ())), preferred_element_type=F32
            ).astype(BF16)


def product_kernel(filt_ref, count_ref, start_ref, data_ref, code_ref, out_ref, rows_ref, dense_ref):
    for comp in range(4):
        for blk in range(8):
            base = comp * TR + blk * DEV
            rows_ref[pl.ds(base, DEV), :] = data_ref[:, base : base + DEV].astype(F32).T
    rows_ref[pl.ds(4 * TR, 8), :] = jnp.zeros((8, DEV), F32)

    def run_cells(run):
        count = count_ref[0, run]
        start = start_ref[0, run]
        code = code_ref[run].astype(I32)
        cols = [(code & 127)[8 * v : 8 * v + 8] for v in range(2)]
        slot = [(code >> 7)[8 * v : 8 * v + 8] for v in range(2)]

        def one_slot(step, acc):
            acc = list(acc)
            for u in range(4):
                j = step * 4 + u
                hit = [slot[v] == j for v in range(2)]
                for comp in range(4):
                    row = jnp.broadcast_to(rows_ref[pl.ds(comp * TR + start + j, 1), :], (8, DEV))
                    for v in range(2):
                        got = jnp.take_along_axis(row, cols[v], axis=1, mode="promise_in_bounds")
                        acc[2 * comp + v] = jnp.where(hit[v], got, acc[2 * comp + v])
            return tuple(acc)

        return lax.fori_loop(0, (count + 3) // 4, one_slot, (jnp.zeros((8, DEV), F32),) * 8)

    top = lax.broadcasted_iota(I32, (8, DEV), 0) < 4

    def two_runs(pair, _):
        even = run_cells(2 * pair)
        odd = run_cells(2 * pair + 1)
        for comp in range(4):
            at = pl.ds(pl.multiple_of(comp * ORDER + pair * 8, 8), 8)
            for v in range(2):
                a, b = even[2 * comp + v], odd[2 * comp + v]
                dense_ref[at, pl.ds(2 * v * DEV, DEV)] = jnp.where(top, a, pltpu.roll(b, 4, 0))
                dense_ref[at, pl.ds((2 * v + 1) * DEV, DEV)] = jnp.where(top, pltpu.roll(a, 4, 0), b)
        return 0

    lax.fori_loop(0, DEV // 2, two_runs, 0)

    mine = lax.axis_index("bin") * 2
    amplitude = 1.0 / math.sqrt(ORDER)
    for i in range(2):
        real = dense_ref[pl.ds(2 * i * ORDER, ORDER), :].astype(BF16)
        imag = dense_ref[pl.ds((2 * i + 1) * ORDER, ORDER), :].astype(BF16)
        fr = filt_ref[0, mine + i]
        fi = filt_ref[1, mine + i]
        for t in range(2):
            cols = slice(t * 256, (t + 1) * 256)
            rc, ic = real[:, cols], imag[:, cols]
            dot = functools.partial(jnp.dot, preferred_element_type=F32)
            sr = dot(real, rc) - dot(imag, ic)
            si = dot(real, ic) + dot(imag, rc)
            outr = ((fr * sr - fi * si) * amplitude).astype(BF16)
            outi = ((fr * si + fi * sr) * amplitude).astype(BF16)
            for b in range(8):
                out_ref[b, 0, i, :, cols] = outr[b * 64 : (b + 1) * 64]
                out_ref[b, 1, i, :, cols] = outi[b * 64 : (b + 1) * 64]


def local(traces, rcv_index, src_index, wave_filter):
    high, low = dft_tables()
    params = pltpu.CompilerParams(vmem_limit_bytes=LIMIT)
    vmem = pl.BlockSpec(memory_space=pltpu.VMEM)
    smem = pl.BlockSpec(memory_space=pltpu.SMEM)
    shape = jax.ShapeDtypeStruct
    order, slots, count, start = pl.pallas_call(
        index_kernel,
        out_shape=(shape((TR, 1), I32), shape((DEV, DEV), BF16), shape((8, DEV), I32), shape((8, DEV), I32)),
        compiler_params=params,
        name="index",
    )(rcv_index.reshape(TR, 1), src_index.reshape(TR, 1))
    slots = lax.all_to_all(slots, ("bin", "freq"), split_axis=0, concat_axis=0, tiled=True)
    steps = 4
    depth = NT // steps
    spectra = pl.pallas_call(
        functools.partial(spectrum_kernel, steps),
        grid=(steps,),
        in_specs=[
            pl.BlockSpec((TR, depth), lambda k: (0, k)),
            pl.BlockSpec((depth, 4 * DEV), lambda k: (k, 0)),
            pl.BlockSpec((depth, 4 * DEV), lambda k: (k, 0)),
            pl.BlockSpec((TR, 1), lambda k: (0, 0)),
        ],
        out_specs=pl.BlockSpec((DEV, 4 * TR), lambda k: (0, 0)),
        out_shape=shape((DEV, 4 * TR), BF16),
        scratch_shapes=[pltpu.VMEM((TR, 4 * DEV), F32)],
        compiler_params=params,
        cost_estimate=pl.CostEstimate(flops=5 * 10**9, bytes_accessed=9 * 10**6, transcendentals=0),
        name="spectrum",
    )(traces, jnp.asarray(high), jnp.asarray(low), order)
    spectra = lax.all_to_all(spectra, ("bin", "freq"), split_axis=0, concat_axis=0, tiled=True)
    code = pl.pallas_call(
        inverse_kernel, out_shape=shape((16, DEV), jnp.int16), compiler_params=params, name="inverse"
    )(slots)
    code = lax.all_gather(code, ("bin", "freq"), axis=0)
    rows = pl.pallas_call(
        product_kernel,
        in_specs=[smem, smem, smem, vmem, vmem],
        out_specs=vmem,
        out_shape=shape((8, 2, 2, 64, ORDER), BF16),
        scratch_shapes=[pltpu.VMEM((4 * TR + 8, DEV), F32), pltpu.VMEM((4 * ORDER, ORDER), F32)],
        compiler_params=params,
        name="product",
    )(wave_filter, count, start, spectra, code)
    rows = lax.all_to_all(rows, "bin", split_axis=0, concat_axis=0, tiled=True)
    return rows.transpose(1, 0, 2, 3, 4).reshape(2, 16, 64, ORDER)


def solution(mesh):
    placed = (P(("bin", "freq"), None), P(("bin", "freq")), P(("bin", "freq")), P(None, "freq"))
    return jax.shard_map(
        local, mesh=mesh, in_specs=placed, out_specs=P(None, "freq", "bin", None), check_vma=False
    )
```

profile of v0, /device:TPU:1, one launch (start us, length us, event | category | flops | bytes accessed | tf_op | source)
XLA Modules:
  0.0 175.5 jit_solution(18034041043086615516)
XLA Ops:
  0.0 1.7 copy.15.rcv_ref
  1.7 1.7 copy.16.src_ref
  3.4 3.4 %index.1 = (s32[1024,1]{1,0:T(8,128)}, bf16[128,128]{1,0:T(8,128)(2,1)}, s32[8,128]{1,0:T(8,128)}, s32[8,128]{1,0:T(8,128)}) custom-call(s32[1024,1]{1,0:T(8,128)} %copy.15.rcv_ref, s32[1024,1]{1,0:T(8,128)} %copy.16.src_ref), custom_call_target="tpu_custom_call" | custom-call | tf_op jit(solution)/shard_map/index/pallas_call | solution.py:178
  6.8 1.4 copy.18
  8.3 11.5 %all-to-all-start.1 = ((bf16[128,1,128]{2,1,0:T(2,128)(2,1)}), bf16[128,1,128]{2,1,0:T(2,128)(2,1)S(1)}, u32[]{:S(2)}, u32[]{:S(2)}) async-start(bf16[128,1,128]{2,1,0:T(2,128)(2,1)} %copy.18), calls=%async_computation.1 | async-start | bytes 131072 | tf_op jit(solution)/shard_map/all_to_all | solution.py:184
  19.8 9.9 %spectrum.1 = bf16[128,4096]{1,0:T(8,128)(2,1)} custom-call(bf16[1024,2048]{1,0:T(8,128)(2,1)} %traces_ref.1, bf16[2048,512]{1,0:T(8,128)(2,1)} %constant.4.clone.high_ref, bf16[2048,512]{1,0:T(8,128)(2,1)} %constant.5.clone.low_ref, s32[1024,1]{1,0:T(8,128)} %get-tuple-element.11.order_ref), custom_call_target="tpu_custom_call" | custom-call | flops 5000000000 | bytes 9000000 | tf_op jit(solution)/shard_map/spectrum/pallas_call | solution.py:187
  29.7 0.6 broadcast
  30.2 2.6 %reduce = bf16[128,4096]{1,0:T(8,128)(2,1)S(1)} reduce(bf16[128,1,4096]{2,0,1:T(8,128)(2,1)} %bitcast.16, bf16[]{:T(256)} %broadcast), dimensions={1}, to_apply=%copy.17.reduce_sub_computation | reduce | bytes 2097154 | tf_op jit(solution)/shard_map/all_to_all | solution.py:203
  32.9 1.6 reshape.17
  34.4 0.0 all-to-all-done.1
  34.5 9.8 %all-to-all-start = ((bf16[128,2,2048]{2,1,0:T(2,128)(2,1)}), bf16[128,2,2048]{2,1,0:T(2,128)(2,1)S(1)}, u32[]{:S(2)}, u32[]{:S(2)}) async-start(bf16[128,2,2048]{2,1,0:T(2,128)(2,1)} %reshape.17), calls=%async_computation | async-start | bytes 2097152 | tf_op jit(solution)/shard_map/all_to_all | solution.py:203
  44.2 0.6 copy.25
  44.8 1.8 %inverse.1 = s16[16,128]{1,0:T(8,128)(2,1)} custom-call(bf16[128,128]{1,0:T(8,128)(2,1)} %bitcast.17), custom_call_target="tpu_custom_call" | custom-call | tf_op jit(solution)/shard_map/inverse/pallas_call | solution.py:204
  46.7 58.9 %all-gather = s16[2048,128]{1,0:T(8,128)(2,1)} all-gather(s16[16,128]{1,0:T(8,128)(2,1)} %inverse.1), channel_id=2, replica_groups=mesh['bin'=8,'freq'=16] {'bin','freq'}, dimensions={0}, use_global_device_ids=true | all-gather | bytes 528384 | tf_op jit(solution)/shard_map/all_gather | solution.py:207
  105.6 0.0 all-to-all-done
  105.6 1.0 reshape.18
  106.7 2.1 %copy.24 = bf16[128,1,4096]{2,0,1:T(8,128)(2,1)} copy(bf16[128,1,4096]{2,1,0:T(2,128)(2,1)S(1)} %reshape.18) | data formatting | bytes 2097152
  108.8 34.5 %product.1 = bf16[8,2,2,64,512]{4,3,2,1,0:T(8,128)(2,1)} custom-call(f32[2,16]{1,0:T(2,128)} %filt_ref.1, s32[8,128]{1,0:T(8,128)} %get-tuple-element.9.count_ref, s32[8,128]{1,0:T(8,128)} %get-tuple-element.10.start_ref, bf16[128,4096]{1,0:T(8,128)(2,1)} %bitcast.14, s16[128,16,128]{2,1,0:T(8,128)(2,1)} %bitcast.15), custom_call_target="tpu_custom_call" | custom-call | tf_op jit(solution)/shard_map/product/pallas_call | solution.py:208
  143.3 30.7 %all_to_all.27 = bf16[8,2,2,64,512]{4,3,2,1,0:T(8,128)(2,1)S(1)} all-to-all(bf16[8,2,2,64,512]{4,3,2,1,0:T(8,128)(2,1)} %product.1), channel_id=1, replica_groups=mesh['bin'=8,'freq'=16] {'bin'}, dimensions={0} | all-to-all | bytes 4194304 | tf_op jit(solution)/shard_map/all_to_all | solution.py:217
  174.0 1.5 copy.19
Async XLA Ops:
  8.3 26.2 %all-to-all-start.1 = ((bf16[128,1,128]{2,1,0:T(2,128)(2,1)}), bf16[128,1,128]{2,1,0:T(2,128)(2,1)S(1)}, u32[]{:S(2)}, u32[]{:S(2)}) async-start(bf16[128,1,128]{2,1,0:T(2,128)(2,1)} %copy.18), calls=%async_computation.1 | async-start | bytes 131072 | tf_op jit(solution)/shard_map/all_to_all | solution.py:184
  34.5 71.1 %all-to-all-start = ((bf16[128,2,2048]{2,1,0:T(2,128)(2,1)}), bf16[128,2,2048]{2,1,0:T(2,128)(2,1)S(1)}, u32[]{:S(2)}, u32[]{:S(2)}) async-start(bf16[128,2,2048]{2,1,0:T(2,128)(2,1)} %reshape.17), calls=%async_computation | async-start | bytes 2097152 | tf_op jit(solution)/shard_map/all_to_all | solution.py:203
where the time goes:
time: 176 us
  blocking collectives  89.6 us (51%)
  Pallas kernels  49.7 us (28%)
  starting transfers between devices  21.3 us (12%)
  local copies, waits for them, and re-layouts  12.3 us (7%)
  other arithmetic  2.61 us (1%)
    all_gather x1, blocking collectives, local(): code = lax.all_gather(code, ('bin', 'freq'), axis=0)  58.9 us
    pallas_call x1, Pallas kernels, local(): pl.pallas_call(product_kernel, in_specs=[smem, smem, smem, vmem, vmem], o...  34.5 us
    all_to_all x1, blocking collectives, local(): rows = lax.all_to_all(rows, 'bin', split_axis=0, concat_axis=0, tiled=True)  30.7 us
    all_to_all x1, starting transfers between devices, local(): lax.all_to_all(slots, ('bin', 'freq'), split_axis=0, concat_axis=0, tiled...  11.5 us
    pallas_call x1, Pallas kernels, local(): pl.pallas_call(functools.partial(spectrum_kernel, steps), grid=(steps,),...  9.91 us
    all_to_all x1, starting transfers between devices, local(): lax.all_to_all(spectra, ('bin', 'freq'), split_axis=0, concat_axis=0, til...  9.76 us
    unnamed x4, local copies, waits for them, and re-layouts  5.36 us
  transfers between devices with their start and end apart: 2, of which 0 were waited for; matrix products, arithmetic and copies ran while one was open for 3% of the time, Pallas kernels for 7%

commit v1 on v0

v1 whole, which is shorter than its diff:
```python
import functools
import math

import jax
import jax.numpy as jnp
import numpy as np
from jax import lax
from jax.experimental import pallas as pl
from jax.experimental.pallas import tpu as pltpu
from jax.sharding import PartitionSpec as P
import ml_dtypes

ORDER = 512
NT = 2048
NF = 256
DEV = 128
TR = 1024
F32 = jnp.float32
BF16 = jnp.bfloat16
I32 = jnp.int32
LIMIT = 56 * 1024 * 1024


def dft_tables():
    comp = np.arange(4)[:, None]
    dev = np.arange(DEV)[None, :]
    freq = ((dev % 16) * 16 + (dev // 16) * 2 + comp // 2).reshape(-1)
    part = np.broadcast_to(comp % 2, (4, DEV)).reshape(-1)
    phase = (np.arange(NT)[:, None] * freq[None, :]) % NT
    angle = 2.0 * np.pi / NT * phase
    table = np.where(part[None, :] == 0, np.cos(angle), -np.sin(angle)) / math.sqrt(NT)
    high = table.astype(ml_dtypes.bfloat16)
    low = (table - high.astype(np.float64)).astype(ml_dtypes.bfloat16)
    return high, low


def index_kernel(rcv_ref, src_ref, order_ref, cell_ref, count_ref, start_ref, list_ref, edge_ref):
    lane = lax.broadcasted_iota(I32, (TR, DEV), 1)
    row_i = lax.broadcasted_iota(I32, (DEV, DEV), 0)
    col_i = lax.broadcasted_iota(I32, (DEV, DEV), 1)
    lower = (col_i < row_i).astype(BF16)
    upper = (row_i < col_i).astype(BF16)
    same = row_i == col_i
    rcv_cols, src_cols = [], []
    for blk in range(TR // DEV):
        for cols, ref in ((rcv_cols, rcv_ref), (src_cols, src_ref)):
            spread = jnp.where(same, jnp.broadcast_to(ref[blk : blk + 1, :], (DEV, DEV)), 0)
            cols.append(jnp.sum(spread.astype(F32), axis=1, keepdims=True).astype(I32))
    rcv = jnp.concatenate(rcv_cols, axis=0)
    src = jnp.concatenate(src_cols, axis=0)
    member = (rcv // 4 == lane).astype(F32)
    carry = jnp.zeros((1, DEV), F32)
    ranks = []
    for blk in range(TR // DEV):
        m = member[blk * DEV : (blk + 1) * DEV]
        ranks.append(jnp.dot(lower, m.astype(BF16), preferred_element_type=F32) + carry)
        carry = carry + jnp.sum(m, axis=0, keepdims=True)
    rank_all = jnp.concatenate(ranks, axis=0)
    counts8 = jnp.broadcast_to(carry, (8, DEV))
    start = jnp.dot(counts8.astype(BF16), upper, preferred_element_type=F32)
    place = jnp.sum(member * (rank_all + start[0:1]), axis=1, keepdims=True).astype(I32)
    order_ref[...] = place
    count_ref[...] = counts8.astype(I32)
    start_ref[...] = start.astype(I32)
    high = ((src // 128) * 4 + rcv % 4).astype(F32)
    low = (src % 128).astype(F32)
    digit = lax.broadcasted_iota(I32, (TR, DEV), 1)
    digits = jnp.where(digit == 0, high, jnp.where(digit == 1, low, 0.0)).astype(BF16)
    pick = (place == lax.broadcasted_iota(I32, (TR, TR), 1)).astype(F32).astype(BF16)
    both = lax.dot_general(digits, pick, (((0,), (0,)), ((), ())), preferred_element_type=F32)
    cell_ref[...] = (both[0:1] * 128.0 + both[1:2]).astype(I32)
    cls = [carry <= 4.0, (carry > 4.0) & (carry <= 8.0), carry > 8.0]
    base = jnp.zeros((1, 1), F32)
    spot = jnp.zeros((1, DEV), F32)
    edges = []
    for kind in cls:
        ind = kind.astype(F32)
        before = jnp.dot(jnp.broadcast_to(ind, (8, DEV)).astype(BF16), upper, preferred_element_type=F32)[0:1]
        spot = spot + ind * (before + base)
        base = base + jnp.sum(ind, axis=1, keepdims=True)
        edges.append(base)
    here = (jnp.broadcast_to(spot, (DEV, DEV)) == row_i.astype(F32)).astype(BF16)
    names = lax.broadcasted_iota(I32, (8, DEV), 1).astype(F32).astype(BF16)
    list_ref[...] = lax.dot_general(
        names, here, (((1,), (1,)), ((), ())), preferred_element_type=F32
    ).astype(I32)
    edge_lane = lax.broadcasted_iota(I32, (8, DEV), 1)
    edge = jnp.where(edge_lane == 0, edges[0], jnp.where(edge_lane == 1, edges[1], edges[2]))
    edge_ref[...] = edge.astype(I32)


def spectrum_kernel(steps, traces_ref, high_ref, low_ref, order_ref, out_ref, acc_ref):
    step = pl.program_id(0)

    @pl.when(step == 0)
    def _():
        acc_ref[...] = jnp.zeros_like(acc_ref)

    x = traces_ref[...]
    acc_ref[...] += jnp.dot(x, high_ref[...], preferred_element_type=F32) + jnp.dot(
        x, low_ref[...], preferred_element_type=F32
    )

    @pl.when(step == steps - 1)
    def _():
        pick = (order_ref[...] == lax.broadcasted_iota(I32, (TR, TR), 1)).astype(F32).astype(BF16)
        for comp in range(4):
            spec = acc_ref[:, comp * DEV : (comp + 1) * DEV].astype(BF16)
            out_ref[:, comp * TR : (comp + 1) * TR] = lax.dot_general(
                spec, pick, (((0,), (0,)), ((), ())), preferred_element_type=F32
            ).astype(BF16)


def product_kernel(
    filt_ref, count_ref, start_ref, list_ref, edge_ref, data_ref, code_ref, out_ref, rows_ref, cell_ref, raw_ref, dense_ref
):
    stride = TR + 16
    for blk in range(8):
        cols = slice(blk * DEV, (blk + 1) * DEV)
        for comp in range(4):
            base = comp * TR + blk * DEV
            rows_ref[pl.ds(comp * stride + blk * DEV, DEV), :] = data_ref[:, base : base + DEV].astype(F32).T
        code = code_ref[:, cols].T
        cell_ref[pl.ds(blk * DEV, DEV), :] = (code // 128).astype(F32)
        cell_ref[pl.ds(stride + blk * DEV, DEV), :] = (code % 128).astype(F32)
    pad = jnp.zeros((16, DEV), F32)
    for comp in range(4):
        rows_ref[pl.ds(comp * stride + TR, 16), :] = pad
    for digit in range(2):
        cell_ref[pl.ds(digit * stride + TR, 16), :] = pad

    sub16 = lax.broadcasted_iota(I32, (16, DEV), 0).astype(F32)
    sub128 = lax.broadcasted_iota(I32, (DEV, DEV), 0).astype(F32).astype(BF16)
    one, zero = jnp.ones((), BF16), jnp.zeros((), BF16)

    def lay_out(run, size):
        count = count_ref[0, run]
        start = start_ref[0, run]
        left, right = [], []
        for j in range(size):
            at = start + j
            high = jnp.broadcast_to(cell_ref[pl.ds(at, 1), :], (16, DEV))
            hit = jnp.where(j < count, high, -1.0) == sub16
            parts = []
            for comp in range(4):
                row = jnp.broadcast_to(rows_ref[pl.ds(comp * stride + at, 1), :], (16, DEV))
                parts.append(jnp.where(hit, row, 0.0).astype(BF16))
            left.append(jnp.concatenate(parts, axis=0))
            low = jnp.broadcast_to(cell_ref[pl.ds(stride + at, 1), :], (16, DEV)).astype(BF16)
            right.append(jnp.where(jnp.concatenate([low] * 8, axis=0) == sub128, one, zero))
        raw_ref[run] = lax.dot_general(
            jnp.concatenate(left, axis=1),
            jnp.concatenate(right, axis=1),
            (((1,), (1,)), ((), ())),
            preferred_element_type=F32,
        )

    begin = 0
    for kind, (size, together) in enumerate(((4, 4), (8, 4), (16, 2))):
        end = edge_ref[0, kind]

        def some_runs(step, _, begin=begin, end=end, size=size, together=together):
            for u in range(together):
                lay_out(list_ref[0, jnp.minimum(begin + step * together + u, end - 1)], size)
            return 0

        lax.fori_loop(0, (end - begin + together - 1) // together, some_runs, 0)
        begin = end

    top = lax.broadcasted_iota(I32, (8, DEV), 0) < 4

    def four_runs(group, _):
        for comp in range(4):
            at = pl.ds(pl.multiple_of(comp * ORDER + group * 16, 16), 16)
            for v in range(2):
                sl = pl.ds(comp * 16 + 8 * v, 8)
                a, b, c, d = [raw_ref[4 * group + u, sl, :] for u in range(4)]
                first = [jnp.where(top, a, pltpu.roll(b, 4, 0)), jnp.where(top, c, pltpu.roll(d, 4, 0))]
                last = [jnp.where(top, pltpu.roll(a, 4, 0), b), jnp.where(top, pltpu.roll(c, 4, 0), d)]
                dense_ref[at, pl.ds(2 * v * DEV, DEV)] = jnp.concatenate(first, axis=0).astype(BF16)
                dense_ref[at, pl.ds((2 * v + 1) * DEV, DEV)] = jnp.concatenate(last, axis=0).astype(BF16)
        return 0

    lax.fori_loop(0, DEV // 4, four_runs, 0, unroll=2)

    mine = lax.axis_index("bin") * 2
    amplitude = 1.0 / math.sqrt(ORDER)
    for i in range(2):
        real = dense_ref[pl.ds(2 * i * ORDER, ORDER), :]
        imag = dense_ref[pl.ds((2 * i + 1) * ORDER, ORDER), :]
        fr = filt_ref[0, mine + i]
        fi = filt_ref[1, mine + i]
        for t in range(2):
            cols = slice(t * 256, (t + 1) * 256)
            rc, ic = real[:, cols], imag[:, cols]
            dot = functools.partial(jnp.dot, preferred_element_type=F32)
            sr = dot(real, rc) - dot(imag, ic)
            si = dot(real, ic) + dot(imag, rc)
            outr = ((fr * sr - fi * si) * amplitude).astype(BF16)
            outi = ((fr * si + fi * sr) * amplitude).astype(BF16)
            for b in range(8):
                out_ref[b, 0, i, :, cols] = outr[b * 64 : (b + 1) * 64]
                out_ref[b, 1, i, :, cols] = outi[b * 64 : (b + 1) * 64]


def local(traces, rcv_index, src_index, wave_filter):
    high, low = dft_tables()
    params = pltpu.CompilerParams(vmem_limit_bytes=LIMIT)
    vmem = pl.BlockSpec(memory_space=pltpu.VMEM)
    smem = pl.BlockSpec(memory_space=pltpu.SMEM)
    shape = jax.ShapeDtypeStruct
    small = shape((8, DEV), I32)
    order, cells, count, start, listed, edge = pl.pallas_call(
        index_kernel,
        out_shape=(shape((TR, 1), I32), shape((1, TR), I32), small, small, small, small),
        compiler_params=params,
        name="index",
    )(rcv_index.reshape(8, DEV), src_index.reshape(8, DEV))
    cells = lax.all_gather(cells, ("bin", "freq"), axis=0, tiled=True)
    steps = 4
    depth = NT // steps
    spectra = pl.pallas_call(
        functools.partial(spectrum_kernel, steps),
        grid=(steps,),
        in_specs=[
            pl.BlockSpec((TR, depth), lambda k: (0, k)),
            pl.BlockSpec((depth, 4 * DEV), lambda k: (k, 0)),
            pl.BlockSpec((depth, 4 * DEV), lambda k: (k, 0)),
            pl.BlockSpec((TR, 1), lambda k: (0, 0)),
        ],
        out_specs=pl.BlockSpec((DEV, 4 * TR), lambda k: (0, 0)),
        out_shape=shape((DEV, 4 * TR), BF16),
        scratch_shapes=[pltpu.VMEM((TR, 4 * DEV), F32)],
        compiler_params=params,
        cost_estimate=pl.CostEstimate(flops=5 * 10**9, bytes_accessed=9 * 10**6, transcendentals=0),
        name="spectrum",
    )(traces, jnp.asarray(high), jnp.asarray(low), order)
    spectra = lax.all_to_all(spectra, ("bin", "freq"), split_axis=0, concat_axis=0, tiled=True)
    rows = pl.pallas_call(
        product_kernel,
        in_specs=[smem, smem, smem, smem, smem, vmem, vmem],
        out_specs=vmem,
        out_shape=shape((8, 2, 2, 64, ORDER), BF16),
        scratch_shapes=[
            pltpu.VMEM((4 * (TR + 16), DEV), F32),
            pltpu.VMEM((2 * (TR + 16), DEV), F32),
            pltpu.VMEM((DEV, 64, DEV), F32),
            pltpu.VMEM((4 * ORDER, ORDER), BF16),
        ],
        compiler_params=params,
        name="product",
    )(wave_filter, count, start, listed, edge, spectra, cells)
    rows = lax.all_to_all(rows, "bin", split_axis=0, concat_axis=0, tiled=True)
    return rows.transpose(1, 0, 2, 3, 4).reshape(2, 16, 64, ORDER)


def solution(mesh):
    placed = (P(("bin", "freq"), None), P(("bin", "freq")), P(("bin", "freq")), P(None, "freq"))
    return jax.shard_map(
        local, mesh=mesh, in_specs=placed, out_specs=P(None, "freq", "bin", None), check_vma=False
    )
```

time: 176 us -> 147 us (0.84)
  Pallas kernels: 49.7 us -> 36.1 us
  starting transfers between devices: 21.3 us -> 11.5 us
  local copies, waits for them, and re-layouts: 12.3 us -> 7.75 us
    pallas_call x3 -> x2, Pallas kernels: 39.8 us -> 26.2 us  [the longest x1 22.7 us: local(): pl.pallas_call(product_kernel, in_specs=[smem, smem, smem, smem, smem, vm...]
    all_to_all x1 -> x0, starting transfers between devices: 11.5 us -> none  [local(): lax.all_to_all(slots, ('bin', 'freq'), split_axis=0, concat_axis=0, tiled...]
    reshape x2 -> x0, local copies, waits for them, and re-layouts: 3.41 us -> none  [the longest x1 1.71 us: local(): src_index.reshape(TR, 1)]
    unnamed x4 -> x6, local copies, waits for them, and re-layouts: 5.36 us -> 5.66 us
  transfers between devices with their start and end apart: 2 -> 1, of which waited for: 0 -> 0; matrix products, arithmetic and copies ran while one was open for 3% -> 1% of each run, Pallas kernels for 7% -> 0%
where the time goes in v1:
time: 147 us; the launch traced here: 146 us
  blocking collectives  88.4 us (60%)
  Pallas kernels  36.1 us (25%)
  starting transfers between devices  11.5 us (8%)
  local copies, waits for them, and re-layouts  7.75 us (5%)
  other arithmetic  2.62 us (2%)
    all_gather x1, blocking collectives, local(): cells = lax.all_gather(cells, ('bin', 'freq'), axis=0, tiled=True)  57.7 us
    all_to_all x1, blocking collectives, local(): rows = lax.all_to_all(rows, 'bin', split_axis=0, concat_axis=0, tiled=True)  30.7 us
    pallas_call x1, Pallas kernels, local(): pl.pallas_call(product_kernel, in_specs=[smem, smem, smem, smem, smem, vm...  22.7 us
    all_to_all x1, starting transfers between devices, local(): lax.all_to_all(spectra, ('bin', 'freq'), split_axis=0, concat_axis=0, til...  11.5 us
    pallas_call x1, Pallas kernels, local(): pl.pallas_call(functools.partial(spectrum_kernel, steps), grid=(steps,),...  9.9 us
    unnamed x6, local copies, waits for them, and re-layouts  5.66 us
    pallas_call x1, Pallas kernels, local(): pl.pallas_call(index_kernel, out_shape=(shape((TR, 1), I32), shape((1, TR...  3.43 us
  transfers between devices with their start and end apart: 1, of which 0 were waited for; matrix products, arithmetic and copies ran while one was open for 1% of the time, Pallas kernels for 0%

profile of v1, /device:TPU:1, one launch (start us, length us, event | category | flops | bytes accessed | tf_op | source)
XLA Modules:
  0.0 146.4 jit_solution(16660260291035036891)
XLA Ops:
  0.0 3.4 %index.1 = (s32[1024,1]{1,0:T(8,128)}, s32[1,1024]{1,0:T(1,128)}, s32[8,128]{1,0:T(8,128)}, s32[8,128]{1,0:T(8,128)}, s32[8,128]{1,0:T(8,128)}, /*index=5*/s32[8,128]{1,0:T(8,128)}) custom-call(s32[8,128]{1,0:T(8,128)} %bitcast.17, s32[8,128]{1,0:T(8,128)} %bitcast.18), custom_call_target="tpu_custom_call" | custom-call | tf_op jit(solution)/shard_map/index/pallas_call | solution.py:213
  3.4 9.9 %spectrum.1 = bf16[128,4096]{1,0:T(8,128)(2,1)} custom-call(bf16[1024,2048]{1,0:T(8,128)(2,1)} %traces_ref.1, bf16[2048,512]{1,0:T(8,128)(2,1)} %constant.4.clone.high_ref, bf16[2048,512]{1,0:T(8,128)(2,1)} %constant.5.clone.low_ref, s32[1024,1]{1,0:T(8,128)} %get-tuple-element.15.order_ref), custom_call_target="tpu_custom_call" | custom-call | flops 5000000000 | bytes 9000000 | tf_op jit(solution)/shard_map/spectrum/pallas_call | solution.py:222
  13.3 0.5 broadcast
  13.9 2.6 %reduce = bf16[128,4096]{1,0:T(8,128)(2,1)S(1)} reduce(bf16[128,1,4096]{2,0,1:T(8,128)(2,1)} %bitcast.15, bf16[]{:T(256)} %broadcast), dimensions={1}, to_apply=%copy.10.reduce_sub_computation | reduce | bytes 2097154 | tf_op jit(solution)/shard_map/all_to_all | solution.py:238
  16.5 0.0 copy-start
  16.5 1.6 %reshape.16 = bf16[128,2,2048]{2,1,0:T(2,128)(2,1)} reshape(bf16[128,4096]{1,0:T(8,128)(2,1)S(1)} %reduce) | data formatting | bytes 2097152
  18.1 11.5 %all-to-all-start = ((bf16[128,2,2048]{2,1,0:T(2,128)(2,1)}), bf16[128,2,2048]{2,1,0:T(2,128)(2,1)S(1)}, u32[]{:S(2)}, u32[]{:S(2)}) async-start(bf16[128,2,2048]{2,1,0:T(2,128)(2,1)} %reshape.16), calls=%async_computation | async-start | bytes 2097152 | tf_op jit(solution)/shard_map/all_to_all | solution.py:238
  29.6 0.0 copy-done
  29.6 57.7 %all-gather = s32[128,1,1024]{2,1,0:T(1,128)S(1)} all-gather(s32[1,1,1024]{2,1,0:T(1,128)S(1)} %bitcast.16), channel_id=1, replica_groups=mesh['bin'=8,'freq'=16] {'bin','freq'}, dimensions={0}, use_global_device_ids=true | all-gather | bytes 528384 | tf_op jit(solution)/shard_map/all_gather | solution.py:219
  87.3 0.9 copy.17
  88.2 0.0 all-to-all-done
  88.2 1.0 reshape.17
  89.3 2.1 %copy.16 = bf16[128,1,4096]{2,0,1:T(8,128)(2,1)} copy(bf16[128,1,4096]{2,1,0:T(2,128)(2,1)S(1)} %reshape.17) | data formatting | bytes 2097152
  91.4 22.7 %product.1 = bf16[8,2,2,64,512]{4,3,2,1,0:T(8,128)(2,1)} custom-call(f32[2,16]{1,0:T(2,128)} %filt_ref.1, s32[8,128]{1,0:T(8,128)} %get-tuple-element.11.count_ref, s32[8,128]{1,0:T(8,128)} %get-tuple-element.12.start_ref, s32[8,128]{1,0:T(8,128)} %get-tuple-element.13.list_ref, s32[8,128]{1,0:T(8,128)} %get-tuple-element.14.edge_ref, ...), custom_call_target="tpu_custom_call" | custom-call | tf_op jit(solution)/shard_map/product/pallas_call | solution.py:239
  114.2 30.7 %all_to_all.16 = bf16[8,2,2,64,512]{4,3,2,1,0:T(8,128)(2,1)S(1)} all-to-all(bf16[8,2,2,64,512]{4,3,2,1,0:T(8,128)(2,1)} %product.1), channel_id=1, replica_groups=mesh['bin'=8,'freq'=16] {'bin'}, dimensions={0} | all-to-all | bytes 4194304 | tf_op jit(solution)/shard_map/all_to_all | solution.py:253
  144.9 1.5 %copy.11 = bf16[2,8,2,64,512]{4,3,2,1,0:T(8,128)(2,1)} copy(bf16[2,8,2,64,512]{4,3,2,0,1:T(8,128)(2,1)S(1)} %bitcast.12) | data formatting | bytes 4194304 | tf_op jit(solution)/shard_map/transpose | solution.py:254
Async XLA Ops:
  16.5 13.1 %copy-start = (s32[1,1024]{1,0:T(1,128)S(1)}, s32[1,1024]{1,0:T(1,128)}, u32[]{:S(2)}) copy-start(s32[1,1024]{1,0:T(1,128)} %get-tuple-element.16) | copy-start | bytes 12292
  18.1 70.2 %all-to-all-start = ((bf16[128,2,2048]{2,1,0:T(2,128)(2,1)}), bf16[128,2,2048]{2,1,0:T(2,128)(2,1)S(1)}, u32[]{:S(2)}, u32[]{:S(2)}) async-start(bf16[128,2,2048]{2,1,0:T(2,128)(2,1)} %reshape.16), calls=%async_computation | async-start | bytes 2097152 | tf_op jit(solution)/shard_map/all_to_all | solution.py:238

commit v2 on v1

--- a/solution.py
+++ b/solution.py
@@ -22,10 +22,11 @@
 
 
 def dft_tables():
-    comp = np.arange(4)[:, None]
-    dev = np.arange(DEV)[None, :]
-    freq = ((dev % 16) * 16 + (dev // 16) * 2 + comp // 2).reshape(-1)
-    part = np.broadcast_to(comp % 2, (4, DEV)).reshape(-1)
+    bins, freqs, part = np.meshgrid(np.arange(8), np.arange(16), np.arange(2), indexing="ij")
+    first = freqs * 16 + bins * 2
+    order = (1, 0, 2)
+    freq = np.concatenate([first.reshape(-1), (first + 1).transpose(order).reshape(-1)])
+    part = np.concatenate([part.reshape(-1), part.transpose(order).reshape(-1)])
     phase = (np.arange(NT)[:, None] * freq[None, :]) % NT
     angle = 2.0 * np.pi / NT * phase
     table = np.where(part[None, :] == 0, np.cos(angle), -np.sin(angle)) / math.sqrt(NT)
@@ -68,7 +69,9 @@
     digits = jnp.where(digit == 0, high, jnp.where(digit == 1, low, 0.0)).astype(BF16)
     pick = (place == lax.broadcasted_iota(I32, (TR, TR), 1)).astype(F32).astype(BF16)
     both = lax.dot_general(digits, pick, (((0,), (0,)), ((), ())), preferred_element_type=F32)
-    cell_ref[...] = (both[0:1] * 128.0 + both[1:2]).astype(I32)
+    for blk in range(TR // DEV):
+        cell_ref[blk : blk + 1, :] = both[0:1, blk * DEV : (blk + 1) * DEV]
+        cell_ref[8 + blk : 9 + blk, :] = both[1:2, blk * DEV : (blk + 1) * DEV]
     cls = [carry <= 4.0, (carry > 4.0) & (carry <= 8.0), carry > 8.0]
     base = jnp.zeros((1, 1), F32)
     spot = jnp.zeros((1, DEV), F32)
@@ -89,12 +92,118 @@
     edge_ref[...] = edge.astype(I32)
 
 
-def spectrum_kernel(steps, traces_ref, high_ref, low_ref, order_ref, out_ref, acc_ref):
+class Exchange:
+    def __init__(self, axis, size, source, target, send, recv):
+        self.axis, self.size, self.source, self.target = axis, size, source, target
+        self.send, self.recv = send, recv
+        self.me = lax.axis_index(axis)
+
+    def copy(self, k):
+        peer = lax.rem(self.me + k, self.size)
+        return pltpu.make_async_remote_copy(
+            src_ref=self.source(peer),
+            dst_ref=self.target(self.me),
+            send_sem=self.send.at[k],
+            recv_sem=self.recv.at[k],
+            device_id={self.axis: peer},
+            device_id_type=pl.DeviceIdType.MESH,
+        )
+
+    def own(self):
+        return pltpu.make_async_copy(self.source(self.me), self.target(self.me), self.recv.at[0])
+
+    def start(self):
+        def step(k, _):
+            self.copy(k).start()
+            return 0
+
+        lax.fori_loop(1, self.size, step, 0)
+        self.own().start()
+
+    def wait_recv(self):
+        def step(k, _):
+            self.copy(k).wait_recv()
+            return 0
+
+        lax.fori_loop(1, self.size, step, 0)
+        self.own().wait()
+
+    def wait_send(self):
+        def step(k, _):
+            self.copy(k).wait_send()
+            return 0
+
+        lax.fori_loop(1, self.size, step, 0)
+
+
+def greet(axes):
+    barrier = pltpu.get_barrier_semaphore()
+    for axis, size in axes:
+        me = lax.axis_index(axis)
+
+        def step(k, _, axis=axis, size=size, me=me):
+            pl.semaphore_signal(
+                barrier, inc=1, device_id={axis: lax.rem(me + k, size)}, device_id_type=pl.DeviceIdType.MESH
+            )
+            return 0
+
+        lax.fori_loop(1, size, step, 0)
+
+
+def spectrum_kernel(
+    steps,
+    traces_ref,
+    high_ref,
+    low_ref,
+    order_ref,
+    cell_ref,
+    data_ref,
+    cells_ref,
+    acc_ref,
+    pick_ref,
+    spread_ref,
+    cell_send,
+    cell_mid,
+    first_send,
+    first_mid,
+    second_send,
+    second_mid,
+    bin_send,
+    bin_recv,
+    freq_send,
+    freq_recv,
+):
     step = pl.program_id(0)
+
+    def over_bin(slot, source, target):
+        return Exchange("bin", 8, source, target, bin_send.at[slot], bin_recv.at[slot])
+
+    def over_freq(slot, source, target):
+        return Exchange("freq", 16, source, target, freq_send.at[slot], freq_recv.at[slot])
+
+    cell_bin = over_bin(0, lambda b: cell_send, lambda me: cell_mid.at[me])
+    cell_freq = over_freq(0, lambda f: cell_mid, lambda me: cells_ref.at[:, me])
+    first_bin = over_bin(1, lambda b: first_send.at[b], lambda me: first_mid.at[me])
+    first_freq = over_freq(1, lambda f: first_mid.at[:, f], lambda me: data_ref.at[:, me, 0])
+    second_freq = over_freq(2, lambda f: second_send.at[f], lambda me: second_mid.at[me])
+    second_bin = over_bin(2, lambda b: second_mid.at[:, b], lambda me: data_ref.at[me, :, 1])
 
     @pl.when(step == 0)
     def _():
+        greet((("bin", 8), ("freq", 16)))
         acc_ref[...] = jnp.zeros_like(acc_ref)
+        cell_send[...] = cell_ref[...].astype(BF16)
+        pick_ref[...] = (order_ref[...] == lax.broadcasted_iota(I32, (TR, TR), 1)).astype(F32).astype(BF16)
+
+    @pl.when(step == 1)
+    def _():
+        pl.semaphore_wait(pltpu.get_barrier_semaphore(), 22)
+        cell_bin.start()
+
+    @pl.when(step == 2)
+    def _():
+        cell_bin.wait_recv()
+        cell_freq.start()
 
     x = traces_ref[...]
     acc_ref[...] += jnp.dot(x, high_ref[...], preferred_element_type=F32) + jnp.dot(
@@ -103,26 +212,48 @@
 
     @pl.when(step == steps - 1)
     def _():
-        pick = (order_ref[...] == lax.broadcasted_iota(I32, (TR, TR), 1)).astype(F32).astype(BF16)
-        for comp in range(4):
-            spec = acc_ref[:, comp * DEV : (comp + 1) * DEV].astype(BF16)
-            out_ref[:, comp * TR : (comp + 1) * TR] = lax.dot_general(
-                spec, pick, (((0,), (0,)), ((), ())), preferred_element_type=F32
-            ).astype(BF16)
-
-
-def product_kernel(
-    filt_ref, count_ref, start_ref, list_ref, edge_ref, data_ref, code_ref, out_ref, rows_ref, cell_ref, raw_ref, dense_ref
+        def sorted_rows(half):
+            spec = acc_ref[:, half * 256 : (half + 1) * 256].astype(BF16)
+            rows = lax.dot_general(
+                spec, pick_ref[...], (((0,), (0,)), ((), ())), preferred_element_type=F32
+            )
+            for blk in range(8):
+                spread_ref[pl.ds(blk, 256, stride=8), :] = rows[:, blk * DEV : (blk + 1) * DEV]
+
+        sorted_rows(0)
+        for b in range(8):
+            first_send[b] = spread_ref[b * 256 : (b + 1) * 256, :].reshape(16, 16, DEV).astype(BF16)
+        first_bin.start()
+        sorted_rows(1)
+        for f in range(16):
+            second_send[f] = spread_ref[f * 128 : (f + 1) * 128, :].reshape(8, 16, DEV).astype(BF16)
+        second_freq.start()
+        first_bin.wait_recv()
+        first_freq.start()
+        second_freq.wait_recv()
+        second_bin.start()
+        cell_freq.wait_recv()
+        first_freq.wait_recv()
+        second_bin.wait_recv()
+        for part in (cell_bin, cell_freq, first_bin, first_freq, second_freq, second_bin):
+            part.wait_send()
+
+
+def layout_kernel(
+    count_ref, start_ref, list_ref, edge_ref, data_ref, code_ref, dense_ref, wide_ref, rows_ref, cell_ref, raw_ref
 ):
     stride = TR + 16
+    for b in range(8):
+        wide_ref[b * 512 : (b + 1) * 512, :] = data_ref[b].reshape(512, DEV).astype(F32)
+        cell_wide = code_ref[b].reshape(256, DEV).astype(F32)
+        wide_ref[4096 + b * 256 : 4096 + (b + 1) * 256, :] = cell_wide
     for blk in range(8):
-        cols = slice(blk * DEV, (blk + 1) * DEV)
         for comp in range(4):
-            base = comp * TR + blk * DEV
-            rows_ref[pl.ds(comp * stride + blk * DEV, DEV), :] = data_ref[:, base : base + DEV].astype(F32).T
-        code = code_ref[:, cols].T
-        cell_ref[pl.ds(blk * DEV, DEV), :] = (code // 128).astype(F32)
-        cell_ref[pl.ds(stride + blk * DEV, DEV), :] = (code % 128).astype(F32)
+            rows_ref[pl.ds(comp * stride + blk * DEV, DEV), :] = wide_ref[pl.ds(comp * 8 + blk, DEV, stride=32), :].T
+        for digit in range(2):
+            cell_ref[pl.ds(digit * stride + blk * DEV, DEV), :] = wide_ref[
+                pl.ds(4096 + digit * 8 + blk, DEV, stride=16), :
+            ].T
     pad = jnp.zeros((16, DEV), F32)
     for comp in range(4):
         rows_ref[pl.ds(comp * stride + TR, 16), :] = pad
@@ -183,8 +314,22 @@
 
     lax.fori_loop(0, DEV // 4, four_runs, 0, unroll=2)
 
+
+def product_kernel(filt_ref, dense_ref, out_ref, block_ref, send, recv):
     mine = lax.axis_index("bin") * 2
     amplitude = 1.0 / math.sqrt(ORDER)
+    greet((("bin", 8),))
+    moves = [
+        Exchange(
+            "bin",
+            8,
+            lambda b, i=i: block_ref.at[b, i],
+            lambda me, i=i: out_ref.at[:, me * 2 + i],
+            send.at[i],
+            recv.at[i],
+        )
+        for i in range(2)
+    ]
     for i in range(2):
         real = dense_ref[pl.ds(2 * i * ORDER, ORDER), :]
         imag = dense_ref[pl.ds((2 * i + 1) * ORDER, ORDER), :]
@@ -199,8 +344,14 @@
             outr = ((fr * sr - fi * si) * amplitude).astype(BF16)
             outi = ((fr * si + fi * sr) * amplitude).astype(BF16)
             for b in range(8):
-                out_ref[b, 0, i, :, cols] = outr[b * 64 : (b + 1) * 64]
-                out_ref[b, 1, i, :, cols] = outi[b * 64 : (b + 1) * 64]
+                block_ref[b, i, 0, :, cols] = outr[b * 64 : (b + 1) * 64]
+                block_ref[b, i, 1, :, cols] = outi[b * 64 : (b + 1) * 64]
+        if i == 0:
+            pl.semaphore_wait(pltpu.get_barrier_semaphore(), 7)
+        moves[i].start()
+    for move in moves:
+        move.wait_recv()
+        move.wait_send()
 
 
 def local(traces, rcv_index, src_index, wave_filter):
@@ -208,18 +359,19 @@
     params = pltpu.CompilerParams(vmem_limit_bytes=LIMIT)
     vmem = pl.BlockSpec(memory_space=pltpu.VMEM)
     smem = pl.BlockSpec(memory_space=pltpu.SMEM)
+    anywhere = pl.BlockSpec(memory_space=pl.ANY)
     shape = jax.ShapeDtypeStruct
     small = shape((8, DEV), I32)
     order, cells, count, start, listed, edge = pl.pallas_call(
         index_kernel,
-        out_shape=(shape((TR, 1), I32), shape((1, TR), I32), small, small, small, small),
+        out_shape=(shape((TR, 1), I32), shape((16, DEV), F32), small, small, small, small),
         compiler_params=params,
         name="index",
     )(rcv_index.reshape(8, DEV), src_index.reshape(8, DEV))
-    cells = lax.all_gather(cells, ("bin", "freq"), axis=0, tiled=True)
     steps = 4
     depth = NT // steps
-    spectra = pl.pallas_call(
+    dma = pltpu.SemaphoreType.DMA
+    data, cells = pl.pallas_call(
         functools.partial(spectrum_kernel, steps),
         grid=(steps,),
         in_specs=[
@@ -227,31 +379,52 @@
             pl.BlockSpec((depth, 4 * DEV), lambda k: (k, 0)),
             pl.BlockSpec((depth, 4 * DEV), lambda k: (k, 0)),
             pl.BlockSpec((TR, 1), lambda k: (0, 0)),
+            pl.BlockSpec((16, DEV), lambda k: (0, 0)),
         ],
-        out_specs=pl.BlockSpec((DEV, 4 * TR), lambda k: (0, 0)),
-        out_shape=shape((DEV, 4 * TR), BF16),
-        scratch_shapes=[pltpu.VMEM((TR, 4 * DEV), F32)],
-        compiler_params=params,
+        out_specs=(anywhere, anywhere),
+        out_shape=(shape((8, 16, 2, 16, DEV), BF16), shape((8, 16, 16, DEV), BF16)),
+        scratch_shapes=[
+            pltpu.VMEM((TR, 4 * DEV), F32),
+            pltpu.VMEM((TR, TR), BF16),
+            pltpu.VMEM((2048, DEV), F32),
+            pltpu.VMEM((16, DEV), BF16),
+            pltpu.VMEM((8, 16, DEV), BF16),
+            pltpu.VMEM((8, 16, 16, DEV), BF16),
+            pltpu.VMEM((8, 16, 16, DEV), BF16),
+            pltpu.VMEM((16, 8, 16, DEV), BF16),
+            pltpu.VMEM((16, 8, 16, DEV), BF16),
+            dma((3, 8)),
+            dma((3, 8)),
+            dma((3, 16)),
+            dma((3, 16)),
+        ],
+        compiler_params=pltpu.CompilerParams(vmem_limit_bytes=LIMIT, collective_id=1, has_side_effects=True),
         cost_estimate=pl.CostEstimate(flops=5 * 10**9, bytes_accessed=9 * 10**6, transcendentals=0),
         name="spectrum",
-    )(traces, jnp.asarray(high), jnp.asarray(low), order)
-    spectra = lax.all_to_all(spectra, ("bin", "freq"), split_axis=0, concat_axis=0, tiled=True)
-    rows = pl.pallas_call(
-        product_kernel,
-        in_specs=[smem, smem, smem, smem, smem, vmem, vmem],
+    )(traces, jnp.asarray(high), jnp.asarray(low), order, cells)
+    dense = pl.pallas_call(
+        layout_kernel,
+        in_specs=[smem, smem, smem, smem, vmem, vmem],
         out_specs=vmem,
-        out_shape=shape((8, 2, 2, 64, ORDER), BF16),
+        out_shape=shape((4 * ORDER, ORDER), BF16),
         scratch_shapes=[
+            pltpu.VMEM((4096 + 2048, DEV), F32),
             pltpu.VMEM((4 * (TR + 16), DEV), F32),
             pltpu.VMEM((2 * (TR + 16), DEV), F32),
             pltpu.VMEM((DEV, 64, DEV), F32),
-            pltpu.VMEM((4 * ORDER, ORDER), BF16),
         ],
         compiler_params=params,
+        name="layout",
+    )(count, start, listed, edge, data, cells)
+    return pl.pallas_call(
+        product_kernel,
+        in_specs=[smem, vmem],
+        out_specs=anywhere,
+        out_shape=shape((2, 16, 64, ORDER), BF16),
+        scratch_shapes=[pltpu.VMEM((8, 2, 2, 64, ORDER), BF16), dma((2, 8)), dma((2, 8))],
+        compiler_params=pltpu.CompilerParams(vmem_limit_bytes=LIMIT, collective_id=2, has_side_effects=True),
         name="product",
-    )(wave_filter, count, start, listed, edge, spectra, cells)
-    rows = lax.all_to_all(rows, "bin", split_axis=0, concat_axis=0, tiled=True)
-    return rows.transpose(1, 0, 2, 3, 4).reshape(2, 16, 64, ORDER)
+    )(wave_filter, dense)
 
 
 def solution(mesh):

time: 147 us -> 95.8 us (0.65)
  blocking collectives: 88.4 us -> 0 us
  Pallas kernels: 36.1 us -> 92.4 us
  starting transfers between devices: 11.5 us -> 0 us
  local copies, waits for them, and re-layouts: 7.75 us -> 3.13 us
  other arithmetic: 2.62 us -> 0 us
    all_gather x1 -> x0, blocking collectives: 57.7 us -> none  [local(): cells = lax.all_gather(cells, ('bin', 'freq'), axis=0, tiled=True)]
    all_to_all x1 -> x0, blocking collectives: 30.7 us -> none  [local(): rows = lax.all_to_all(rows, 'bin', split_axis=0, concat_axis=0, tiled=True)]
    pallas_call x1, Pallas kernels: 9.9 us -> 39 us  [local(): pl.pallas_call(functools.partial(spectrum_kernel, steps), grid=(steps,),...]
    pallas_call x2 -> x3, Pallas kernels: 26.2 us -> 53.4 us  [the longest x1 28.5 us: local(): pl.pallas_call(product_kernel, in_specs=[smem, vmem], out_specs=anywhere,...]
    all_to_all x1 -> x0, starting transfers between devices: 11.5 us -> none  [local(): lax.all_to_all(spectra, ('bin', 'freq'), split_axis=0, concat_axis=0, til...]
    all_to_all x1 -> x0, other arithmetic: 2.62 us -> none  [local(): lax.all_to_all(spectra, ('bin', 'freq'), split_axis=0, concat_axis=0, til...]
    unnamed x6 -> x1, local copies, waits for them, and re-layouts: 5.66 us -> 3.13 us
    transpose x1 -> x0, local copies, waits for them, and re-layouts: 1.55 us -> none  [local(): return rows.transpose(1, 0, 2, 3, 4).reshape(2, 16, 64, ORDER)]
  transfers between devices with their start and end apart: 1 -> 0, of which waited for: 0 -> 0; matrix products, arithmetic and copies ran while one was open for 1% -> 0% of each run, Pallas kernels for 0% -> 0%
where the time goes in v2:
time: 95.8 us; the launch traced here: 95.5 us
  Pallas kernels  92.4 us (96%)
  local copies, waits for them, and re-layouts  3.13 us (3%)
    pallas_call x1, Pallas kernels, local(): pl.pallas_call(functools.partial(spectrum_kernel, steps), grid=(steps,),...  39 us
    pallas_call x1, Pallas kernels, local(): pl.pallas_call(product_kernel, in_specs=[smem, vmem], out_specs=anywhere,...  28.5 us
    pallas_call x1, Pallas kernels, local(): pl.pallas_call(layout_kernel, in_specs=[smem, smem, smem, smem, vmem, vme...  21.4 us
    pallas_call x1, Pallas kernels, local(): pl.pallas_call(index_kernel, out_shape=(shape((TR, 1), I32), shape((16, D...  3.43 us
    unnamed x1, local copies, waits for them, and re-layouts  3.13 us

profile of v2, /device:TPU:1, one launch (start us, length us, event | category | flops | bytes accessed | tf_op | source)
XLA Modules:
  0.0 95.5 jit_solution(12471648498449673152)
XLA Ops:
  0.0 3.4 %index.1 = (s32[1024,1]{1,0:T(8,128)}, f32[16,128]{1,0:T(8,128)}, s32[8,128]{1,0:T(8,128)}, s32[8,128]{1,0:T(8,128)}, s32[8,128]{1,0:T(8,128)}, /*index=5*/s32[8,128]{1,0:T(8,128)}) custom-call(s32[8,128]{1,0:T(8,128)} %bitcast.2, s32[8,128]{1,0:T(8,128)} %bitcast.3), custom_call_target="tpu_custom_call" | custom-call | tf_op jit(solution)/shard_map/index/pallas_call | solution.py:365
  3.4 39.0 %spectrum.1 = (bf16[8,16,2,16,128]{4,3,2,1,0:T(8,128)(2,1)}, bf16[8,16,16,128]{3,2,1,0:T(8,128)(2,1)}) custom-call(bf16[1024,2048]{1,0:T(8,128)(2,1)} %traces_ref.1, bf16[2048,512]{1,0:T(8,128)(2,1)} %constant.4.clone.high_ref, bf16[2048,512]{1,0:T(8,128)(2,1)} %constant.5.clone.low_ref, s32[1024,1]{1,0:T(8,128)} %get-tuple-element.17.order_ref, ...), custom_call_target="tpu_custom_call" | custom-call | flops 5000000000 | bytes 9000000 | tf_op jit(solution)/shard_map/spectrum/pallas_call | solution.py:374
  42.5 21.4 %layout.1.dense_ref = bf16[2048,512]{1,0:T(8,128)(2,1)} custom-call(s32[8,128]{1,0:T(8,128)} %get-tuple-element.13.count_ref, s32[8,128]{1,0:T(8,128)} %get-tuple-element.14.start_ref, s32[8,128]{1,0:T(8,128)} %get-tuple-element.15.list_ref, s32[8,128]{1,0:T(8,128)} %get-tuple-element.16.edge_ref, bf16[8,16,2,16,128]{4,3,2,1,0:T(8,128)(2,1)} %get-tuple-element.19.data_ref, ...), custom_call_target="tpu_custom_call" | custom-call | tf_op jit(solution)/shard_map/layout/pallas_call | solution.py:405
  63.9 28.5 %product.1 = bf16[2,16,64,512]{3,2,1,0:T(8,128)(2,1)} custom-call(f32[2,16]{1,0:T(2,128)} %filt_ref.1, bf16[2048,512]{1,0:T(8,128)(2,1)} %layout.1.dense_ref), custom_call_target="tpu_custom_call" | custom-call | tf_op jit(solution)/shard_map/product/pallas_call | solution.py:419
  92.4 3.1 %copy.8 = bf16[2,16,64,512]{3,2,1,0:T(8,128)(2,1)} copy(bf16[2,16,64,512]{3,2,1,0:T(8,128)(2,1)} %product.1) | data formatting | bytes 4194304

commit v3 on v2

--- a/solution.py
+++ b/solution.py
@@ -32,10 +32,10 @@
     table = np.where(part[None, :] == 0, np.cos(angle), -np.sin(angle)) / math.sqrt(NT)
     high = table.astype(ml_dtypes.bfloat16)
     low = (table - high.astype(np.float64)).astype(ml_dtypes.bfloat16)
-    return high, low
-
-
-def index_kernel(rcv_ref, src_ref, order_ref, cell_ref, count_ref, start_ref, list_ref, edge_ref):
+    return [np.concatenate([high[:, h : h + 256], low[:, h : h + 256]], axis=1) for h in (0, 256)]
+
+
+def index_work(rcv_ref, src_ref, pick_ref, cell_ref, spread_ref, count_ref, start_ref):
     lane = lax.broadcasted_iota(I32, (TR, DEV), 1)
     row_i = lax.broadcasted_iota(I32, (DEV, DEV), 0)
     col_i = lax.broadcasted_iota(I32, (DEV, DEV), 1)
@@ -60,18 +60,22 @@
     counts8 = jnp.broadcast_to(carry, (8, DEV))
     start = jnp.dot(counts8.astype(BF16), upper, preferred_element_type=F32)
     place = jnp.sum(member * (rank_all + start[0:1]), axis=1, keepdims=True).astype(I32)
-    order_ref[...] = place
     count_ref[...] = counts8.astype(I32)
     start_ref[...] = start.astype(I32)
     high = ((src // 128) * 4 + rcv % 4).astype(F32)
     low = (src % 128).astype(F32)
     digit = lax.broadcasted_iota(I32, (TR, DEV), 1)
     digits = jnp.where(digit == 0, high, jnp.where(digit == 1, low, 0.0)).astype(BF16)
-    pick = (place == lax.broadcasted_iota(I32, (TR, TR), 1)).astype(F32).astype(BF16)
-    both = lax.dot_general(digits, pick, (((0,), (0,)), ((), ())), preferred_element_type=F32)
+    pick_ref[...] = (place == lax.broadcasted_iota(I32, (TR, TR), 1)).astype(F32).astype(BF16)
+    both = lax.dot_general(digits, pick_ref[...], (((0,), (0,)), ((), ())), preferred_element_type=F32)
     for blk in range(TR // DEV):
-        cell_ref[blk : blk + 1, :] = both[0:1, blk * DEV : (blk + 1) * DEV]
-        cell_ref[8 + blk : 9 + blk, :] = both[1:2, blk * DEV : (blk + 1) * DEV]
+        spread_ref[blk : blk + 1, :] = both[0:1, blk * DEV : (blk + 1) * DEV]
+        spread_ref[8 + blk : 9 + blk, :] = both[1:2, blk * DEV : (blk + 1) * DEV]
+    cell_ref[...] = spread_ref[0:16, :].astype(BF16)
+    return carry, upper, row_i
+
+
+def list_runs(carry, upper, row_i, list_ref, edge_ref):
     cls = [carry <= 4.0, (carry > 4.0) & (carry <= 8.0), carry > 8.0]
     base = jnp.zeros((1, 1), F32)
     spot = jnp.zeros((1, DEV), F32)
@@ -151,16 +155,22 @@
 
 
 def spectrum_kernel(
-    steps,
+    rcv_ref,
+    src_ref,
     traces_ref,
-    high_ref,
-    low_ref,
-    order_ref,
-    cell_ref,
-    data_ref,
+    first_ref,
+    second_ref,
+    data_first_ref,
+    data_second_ref,
     cells_ref,
-    acc_ref,
+    count_ref,
+    start_ref,
+    list_ref,
+    edge_ref,
+    x_ref,
+    table_ref,
     pick_ref,
+    spec_ref,
     spread_ref,
     cell_send,
     cell_mid,
@@ -168,13 +178,12 @@
     first_mid,
     second_send,
     second_mid,
+    load_sem,
     bin_send,
     bin_recv,
     freq_send,
     freq_recv,
 ):
-    step = pl.program_id(0)
-
     def over_bin(slot, source, target):
         return Exchange("bin", 8, source, target, bin_send.at[slot], bin_recv.at[slot])
 
@@ -182,78 +191,103 @@
         return Exchange("freq", 16, source, target, freq_send.at[slot], freq_recv.at[slot])
 
     cell_bin = over_bin(0, lambda b: cell_send, lambda me: cell_mid.at[me])
-    cell_freq = over_freq(0, lambda f: cell_mid, lambda me: cells_ref.at[:, me])
+    cell_freq = over_freq(0, lambda f: cell_mid, lambda me: cells_ref.at[me])
     first_bin = over_bin(1, lambda b: first_send.at[b], lambda me: first_mid.at[me])
-    first_freq = over_freq(1, lambda f: first_mid.at[:, f], lambda me: data_ref.at[:, me, 0])
+    first_freq = over_freq(1, lambda f: first_mid.at[:, f], lambda me: data_first_ref.at[me])
     second_freq = over_freq(2, lambda f: second_send.at[f], lambda me: second_mid.at[me])
-    second_bin = over_bin(2, lambda b: second_mid.at[:, b], lambda me: data_ref.at[me, :, 1])
-
-    @pl.when(step == 0)
-    def _():
-        greet((("bin", 8), ("freq", 16)))
-        acc_ref[...] = jnp.zeros_like(acc_ref)
-        cell_send[...] = cell_ref[...].astype(BF16)
-        pick_ref[...] = (order_ref[...] == lax.broadcasted_iota(I32, (TR, TR), 1)).astype(F32).astype(BF16)
-
-    @pl.when(step == 1)
-    def _():
-        pl.semaphore_wait(pltpu.get_barrier_semaphore(), 22)
-        cell_bin.start()
-
-    @pl.when(step == 2)
-    def _():
-        cell_bin.wait_recv()
-        cell_freq.start()
-
-    x = traces_ref[...]
-    acc_ref[...] += jnp.dot(x, high_ref[...], preferred_element_type=F32) + jnp.dot(
-        x, low_ref[...], preferred_element_type=F32
-    )
-
-    @pl.when(step == steps - 1)
-    def _():
-        def sorted_rows(half):
-            spec = acc_ref[:, half * 256 : (half + 1) * 256].astype(BF16)
+    second_bin = over_bin(2, lambda b: second_mid.at[:, b], lambda me: data_second_ref.at[me])
+
+    def load_traces(m):
+        at = pl.ds(m * 256, 256)
+        return pltpu.make_async_copy(traces_ref.at[at], x_ref.at[at], load_sem.at[m])
+
+    def load_table(h):
+        return pltpu.make_async_copy((first_ref, second_ref)[h], table_ref.at[h], load_sem.at[4 + h])
+
+    greet((("bin", 8), ("freq", 16)))
+    load_table(0).start()
+    for m in range(4):
+        load_traces(m).start()
+    load_table(1).start()
+    carry, upper, row_i = index_work(rcv_ref, src_ref, pick_ref, cell_send, spread_ref, count_ref, start_ref)
+    pl.semaphore_wait(pltpu.get_barrier_semaphore(), 22)
+    cell_bin.start()
+    list_runs(carry, upper, row_i, list_ref, edge_ref)
+
+    def transform(h):
+        load_table(h).wait()
+
+        def rows(m, _):
+            if h == 0:
+                load_traces(m).wait()
+            at = pl.ds(pl.multiple_of(m * 256, 256), 256)
+            both = jnp.dot(x_ref[at, :], table_ref[h], preferred_element_type=F32)
+            spec_ref[at, :] = (both[:, :256] + both[:, 256:]).astype(BF16)
+            return 0
+
+        lax.fori_loop(0, 4, rows, 0)
+
+    def sort_rows():
+        for half in range(2):
+            q = half * 512
             rows = lax.dot_general(
-                spec, pick_ref[...], (((0,), (0,)), ((), ())), preferred_element_type=F32
+                spec_ref[...], pick_ref[:, q : q + 512], (((0,), (0,)), ((), ())), preferred_element_type=F32
             )
-            for blk in range(8):
-                spread_ref[pl.ds(blk, 256, stride=8), :] = rows[:, blk * DEV : (blk + 1) * DEV]
-
-        sorted_rows(0)
-        for b in range(8):
-            first_send[b] = spread_ref[b * 256 : (b + 1) * 256, :].reshape(16, 16, DEV).astype(BF16)
-        first_bin.start()
-        sorted_rows(1)
-        for f in range(16):
-            second_send[f] = spread_ref[f * 128 : (f + 1) * 128, :].reshape(8, 16, DEV).astype(BF16)
-        second_freq.start()
-        first_bin.wait_recv()
-        first_freq.start()
-        second_freq.wait_recv()
-        second_bin.start()
-        cell_freq.wait_recv()
-        first_freq.wait_recv()
-        second_bin.wait_recv()
-        for part in (cell_bin, cell_freq, first_bin, first_freq, second_freq, second_bin):
-            part.wait_send()
+            for blk in range(4):
+                spread_ref[pl.ds(half * 4 + blk, 256, stride=8), :] = rows[:, blk * DEV : (blk + 1) * DEV]
+
+    transform(0)
+    cell_bin.wait_recv()
+    cell_freq.start()
+    sort_rows()
+    for b in range(8):
+        first_send[b] = spread_ref[b * 256 : (b + 1) * 256, :].reshape(16, 16, DEV).astype(BF16)
+    first_bin.start()
+    transform(1)
+    sort_rows()
+    for f in range(16):
+        second_send[f] = spread_ref[f * 128 : (f + 1) * 128, :].reshape(8, 16, DEV).astype(BF16)
+    second_freq.start()
+    first_bin.wait_recv()
+    first_freq.start()
+    second_freq.wait_recv()
+    second_bin.start()
+    cell_freq.wait_recv()
+    first_freq.wait_recv()
+    second_bin.wait_recv()
+    for part in (cell_bin, cell_freq, first_bin, first_freq, second_freq, second_bin):
+        part.wait_send()
 
 
 def layout_kernel(
-    count_ref, start_ref, list_ref, edge_ref, data_ref, code_ref, dense_ref, wide_ref, rows_ref, cell_ref, raw_ref
+    count_ref,
+    start_ref,
+    list_ref,
+    edge_ref,
+    first_ref,
+    second_ref,
+    code_ref,
+    dense_ref,
+    first_wide,
+    second_wide,
+    code_wide,
+    rows_ref,
+    cell_ref,
+    raw_ref,
 ):
     stride = TR + 16
     for b in range(8):
-        wide_ref[b * 512 : (b + 1) * 512, :] = data_ref[b].reshape(512, DEV).astype(F32)
-        cell_wide = code_ref[b].reshape(256, DEV).astype(F32)
-        wide_ref[4096 + b * 256 : 4096 + (b + 1) * 256, :] = cell_wide
+        second_wide[b * 256 : (b + 1) * 256, :] = second_ref[b].reshape(256, DEV).astype(F32)
+        for f in range(16):
+            at = (b * 16 + f) * 16
+            first_wide[at : at + 16, :] = first_ref[f, b].astype(F32)
+            code_wide[at : at + 16, :] = code_ref[f, b].astype(F32)
     for blk in range(8):
-        for comp in range(4):
-            rows_ref[pl.ds(comp * stride + blk * DEV, DEV), :] = wide_ref[pl.ds(comp * 8 + blk, DEV, stride=32), :].T
-        for digit in range(2):
-            cell_ref[pl.ds(digit * stride + blk * DEV, DEV), :] = wide_ref[
-                pl.ds(4096 + digit * 8 + blk, DEV, stride=16), :
-            ].T
+        for part in range(2):
+            pick = pl.ds(part * 8 + blk, DEV, stride=16)
+            rows_ref[pl.ds(part * stride + blk * DEV, DEV), :] = first_wide[pick, :].T
+            rows_ref[pl.ds((2 + part) * stride + blk * DEV, DEV), :] = second_wide[pick, :].T
+            cell_ref[pl.ds(part * stride + blk * DEV, DEV), :] = code_wide[pick, :].T
     pad = jnp.zeros((16, DEV), F32)
     for comp in range(4):
         rows_ref[pl.ds(comp * stride + TR, 16), :] = pad
@@ -355,44 +389,41 @@
 
 
 def local(traces, rcv_index, src_index, wave_filter):
-    high, low = dft_tables()
+    tables = dft_tables()
     params = pltpu.CompilerParams(vmem_limit_bytes=LIMIT)
     vmem = pl.BlockSpec(memory_space=pltpu.VMEM)
     smem = pl.BlockSpec(memory_space=pltpu.SMEM)
     anywhere = pl.BlockSpec(memory_space=pl.ANY)
     shape = jax.ShapeDtypeStruct
     small = shape((8, DEV), I32)
-    order, cells, count, start, listed, edge = pl.pallas_call(
-        index_kernel,
-        out_shape=(shape((TR, 1), I32), shape((16, DEV), F32), small, small, small, small),
-        compiler_params=params,
-        name="index",
-    )(rcv_index.reshape(8, DEV), src_index.reshape(8, DEV))
-    steps = 4
-    depth = NT // steps
     dma = pltpu.SemaphoreType.DMA
-    data, cells = pl.pallas_call(
-        functools.partial(spectrum_kernel, steps),
-        grid=(steps,),
-        in_specs=[
-            pl.BlockSpec((TR, depth), lambda k: (0, k)),
-            pl.BlockSpec((depth, 4 * DEV), lambda k: (k, 0)),
-            pl.BlockSpec((depth, 4 * DEV), lambda k: (k, 0)),
-            pl.BlockSpec((TR, 1), lambda k: (0, 0)),
-            pl.BlockSpec((16, DEV), lambda k: (0, 0)),
-        ],
-        out_specs=(anywhere, anywhere),
-        out_shape=(shape((8, 16, 2, 16, DEV), BF16), shape((8, 16, 16, DEV), BF16)),
+    outgoing, middle = pltpu.VMEM((8, 16, 16, DEV), BF16), pltpu.VMEM((16, 8, 16, DEV), BF16)
+    first, second, cells, count, start, listed, edge = pl.pallas_call(
+        spectrum_kernel,
+        in_specs=[vmem, vmem, anywhere, anywhere, anywhere],
+        out_specs=(anywhere, anywhere, anywhere, vmem, vmem, vmem, vmem),
+        out_shape=(
+            shape((16, 8, 16, DEV), BF16),
+            shape((8, 16, 16, DEV), BF16),
+            shape((16, 8, 16, DEV), BF16),
+            small,
+            small,
+            small,
+            small,
+        ),
         scratch_shapes=[
-            pltpu.VMEM((TR, 4 * DEV), F32),
+            pltpu.VMEM((TR, NT), BF16),
+            pltpu.VMEM((2, NT, 4 * DEV), BF16),
             pltpu.VMEM((TR, TR), BF16),
+            pltpu.VMEM((TR, 256), BF16),
             pltpu.VMEM((2048, DEV), F32),
             pltpu.VMEM((16, DEV), BF16),
             pltpu.VMEM((8, 16, DEV), BF16),
-            pltpu.VMEM((8, 16, 16, DEV), BF16),
-            pltpu.VMEM((8, 16, 16, DEV), BF16),
-            pltpu.VMEM((16, 8, 16, DEV), BF16),
-            pltpu.VMEM((16, 8, 16, DEV), BF16),
+            outgoing,
+            outgoing,
+            middle,
+            middle,
+            dma((6,)),
             dma((3, 8)),
             dma((3, 8)),
             dma((3, 16)),
@@ -401,21 +432,23 @@
         compiler_params=pltpu.CompilerParams(vmem_limit_bytes=LIMIT, collective_id=1, has_side_effects=True),
         cost_estimate=pl.CostEstimate(flops=5 * 10**9, bytes_accessed=9 * 10**6, transcendentals=0),
         name="spectrum",
-    )(traces, jnp.asarray(high), jnp.asarray(low), order, cells)
+    )(rcv_index.reshape(8, DEV), src_index.reshape(8, DEV), traces, jnp.asarray(tables[0]), jnp.asarray(tables[1]))
     dense = pl.pallas_call(
         layout_kernel,
-        in_specs=[smem, smem, smem, smem, vmem, vmem],
+        in_specs=[smem, smem, smem, smem, vmem, vmem, vmem],
         out_specs=vmem,
         out_shape=shape((4 * ORDER, ORDER), BF16),
         scratch_shapes=[
-            pltpu.VMEM((4096 + 2048, DEV), F32),
+            pltpu.VMEM((2048, DEV), F32),
+            pltpu.VMEM((2048, DEV), F32),
+            pltpu.VMEM((2048, DEV), F32),
             pltpu.VMEM((4 * (TR + 16), DEV), F32),
             pltpu.VMEM((2 * (TR + 16), DEV), F32),
             pltpu.VMEM((DEV, 64, DEV), F32),
         ],
         compiler_params=params,
         name="layout",
-    )(count, start, listed, edge, data, cells)
+    )(count, start, listed, edge, first, second, cells)
     return pl.pallas_call(
         product_kernel,
         in_specs=[smem, vmem],

time: 95.8 us -> 92.7 us (0.968)
  Pallas kernels: 92.4 us -> 89.4 us
    pallas_call x2 -> x1, Pallas kernels: 42.5 us -> 39.4 us  [local(): pl.pallas_call(spectrum_kernel, in_specs=[vmem, vmem, anywhere, anywhere,...]
where the time goes in v3:
time: 92.7 us; the launch traced here: 92.5 us
  Pallas kernels  89.4 us (96%)
  local copies, waits for them, and re-layouts  3.13 us (3%)
    pallas_call x1, Pallas kernels, local(): pl.pallas_call(spectrum_kernel, in_specs=[vmem, vmem, anywhere, anywhere,...  39.4 us
    pallas_call x1, Pallas kernels, local(): pl.pallas_call(product_kernel, in_specs=[smem, vmem], out_specs=anywhere,...  28.8 us
    pallas_call x1, Pallas kernels, local(): pl.pallas_call(layout_kernel, in_specs=[smem, smem, smem, smem, vmem, vme...  21.1 us
    unnamed x1, local copies, waits for them, and re-layouts  3.13 us

profile of v3, /device:TPU:1, one launch (start us, length us, event | category | flops | bytes accessed | tf_op | source)
XLA Modules:
  0.0 92.5 jit_solution(8530652849692035262)
XLA Ops:
  0.0 39.4 %spectrum.1 = (bf16[16,8,16,128]{3,2,1,0:T(8,128)(2,1)}, bf16[8,16,16,128]{3,2,1,0:T(8,128)(2,1)}, bf16[16,8,16,128]{3,2,1,0:T(8,128)(2,1)}, s32[8,128]{1,0:T(8,...) custom-call(s32[8,128]{1,0:T(8,128)} %bitcast.2, s32[8,128]{1,0:T(8,128)} %bitcast.3, ...), custom_call_target="tpu_custom_call" | custom-call | flops 5000000000 | bytes 9000000 | tf_op jit(solution)/shard_map/spectrum/pallas_call | solution.py:401
  39.4 21.1 %layout.1.dense_ref = bf16[2048,512]{1,0:T(8,128)(2,1)} custom-call(s32[8,128]{1,0:T(8,128)} %get-tuple-element.12.count_ref, s32[8,128]{1,0:T(8,128)} %get-tuple-element.13.start_ref, s32[8,128]{1,0:T(8,128)} %get-tuple-element.14.list_ref, s32[8,128]{1,0:T(8,128)} %get-tuple-element.15.edge_ref, bf16[16,8,16,128]{3,2,1,0:T(8,128)(2,1)} %get-tuple-element.16.first_ref, ...), custom_call_target="tpu_custom_call" | custom-call | tf_op jit(solution)/shard_map/layout/pallas_call | solution.py:436
  60.5 28.8 %product.1 = bf16[2,16,64,512]{3,2,1,0:T(8,128)(2,1)} custom-call(f32[2,16]{1,0:T(2,128)} %filt_ref.1, bf16[2048,512]{1,0:T(8,128)(2,1)} %layout.1.dense_ref), custom_call_target="tpu_custom_call" | custom-call | tf_op jit(solution)/shard_map/product/pallas_call | solution.py:452
  89.4 3.1 %copy.8 = bf16[2,16,64,512]{3,2,1,0:T(8,128)(2,1)} copy(bf16[2,16,64,512]{3,2,1,0:T(8,128)(2,1)} %product.1) | data formatting | bytes 4194304

commit v4 on v3

--- a/solution.py
+++ b/solution.py
@@ -35,7 +35,7 @@
     return [np.concatenate([high[:, h : h + 256], low[:, h : h + 256]], axis=1) for h in (0, 256)]
 
 
-def index_work(rcv_ref, src_ref, pick_ref, cell_ref, spread_ref, count_ref, start_ref):
+def index_work(rcv_ref, src_ref, pick_ref, cell_ref, count_ref, start_ref):
     lane = lax.broadcasted_iota(I32, (TR, DEV), 1)
     row_i = lax.broadcasted_iota(I32, (DEV, DEV), 0)
     col_i = lax.broadcasted_iota(I32, (DEV, DEV), 1)
@@ -62,16 +62,16 @@
     place = jnp.sum(member * (rank_all + start[0:1]), axis=1, keepdims=True).astype(I32)
     count_ref[...] = counts8.astype(I32)
     start_ref[...] = start.astype(I32)
-    high = ((src // 128) * 4 + rcv % 4).astype(F32)
-    low = (src % 128).astype(F32)
+    half = (src // 64 + rcv // 4) % 2
+    high = ((src // 128) * 8 + half * 4 + rcv % 4).astype(F32)
+    low = (src % 64).astype(F32)
     digit = lax.broadcasted_iota(I32, (TR, DEV), 1)
     digits = jnp.where(digit == 0, high, jnp.where(digit == 1, low, 0.0)).astype(BF16)
     pick_ref[...] = (place == lax.broadcasted_iota(I32, (TR, TR), 1)).astype(F32).astype(BF16)
     both = lax.dot_general(digits, pick_ref[...], (((0,), (0,)), ((), ())), preferred_element_type=F32)
     for blk in range(TR // DEV):
-        spread_ref[blk : blk + 1, :] = both[0:1, blk * DEV : (blk + 1) * DEV]
-        spread_ref[8 + blk : 9 + blk, :] = both[1:2, blk * DEV : (blk + 1) * DEV]
-    cell_ref[...] = spread_ref[0:16, :].astype(BF16)
+        cols = slice(blk * DEV, (blk + 1) * DEV)
+        cell_ref[blk : blk + 1, :] = (both[0:1, cols] * 64.0 + both[1:2, cols]).astype(I32)
     return carry, upper, row_i
 
 
@@ -97,13 +97,14 @@
 
 
 class Exchange:
-    def __init__(self, axis, size, source, target, send, recv):
+    def __init__(self, axis, size, source, target, send, recv, peers=None, keep=True):
         self.axis, self.size, self.source, self.target = axis, size, source, target
-        self.send, self.recv = send, recv
+        self.send, self.recv, self.keep = send, recv, keep
         self.me = lax.axis_index(axis)
+        self.peers = peers if peers is not None else lambda k: lax.rem(self.me + k, size)
 
     def copy(self, k):
-        peer = lax.rem(self.me + k, self.size)
+        peer = self.peers(k)
         return pltpu.make_async_remote_copy(
             src_ref=self.source(peer),
             dst_ref=self.target(self.me),
@@ -122,7 +123,8 @@
             return 0
 
         lax.fori_loop(1, self.size, step, 0)
-        self.own().start()
+        if self.keep:
+            self.own().start()
 
     def wait_recv(self):
         def step(k, _):
@@ -130,7 +132,8 @@
             return 0
 
         lax.fori_loop(1, self.size, step, 0)
-        self.own().wait()
+        if self.keep:
+            self.own().wait()
 
     def wait_send(self):
         def step(k, _):
@@ -162,7 +165,7 @@
     second_ref,
     data_first_ref,
     data_second_ref,
-    cells_ref,
+    cell_rows_ref,
     count_ref,
     start_ref,
     list_ref,
@@ -174,6 +177,9 @@
     spread_ref,
     cell_send,
     cell_mid,
+    cell_pack,
+    cell_all,
+    code_wide,
     first_send,
     first_mid,
     second_send,
@@ -183,6 +189,8 @@
     bin_recv,
     freq_send,
     freq_recv,
+    core_send,
+    core_recv,
 ):
     def over_bin(slot, source, target):
         return Exchange("bin", 8, source, target, bin_send.at[slot], bin_recv.at[slot])
@@ -190,8 +198,28 @@
     def over_freq(slot, source, target):
         return Exchange("freq", 16, source, target, freq_send.at[slot], freq_recv.at[slot])
 
-    cell_bin = over_bin(0, lambda b: cell_send, lambda me: cell_mid.at[me])
-    cell_freq = over_freq(0, lambda f: cell_mid, lambda me: cells_ref.at[me])
+    bin_me = lax.axis_index("bin")
+    core, x_me = lax.rem(bin_me, 2), bin_me // 2
+    cell_freq = over_freq(0, lambda f: cell_send, lambda me: cell_mid.at[me])
+    cell_x = Exchange(
+        "bin",
+        4,
+        lambda b: cell_pack,
+        lambda me: cell_all.at[core, x_me],
+        bin_send.at[0],
+        bin_recv.at[0],
+        peers=lambda k: lax.rem(bin_me + 2 * k, 8),
+    )
+    cell_core = Exchange(
+        "bin",
+        2,
+        lambda b: cell_all.at[core],
+        lambda me: cell_all.at[core],
+        core_send,
+        core_recv,
+        peers=lambda k: bin_me + 1 - 2 * core,
+        keep=False,
+    )
     first_bin = over_bin(1, lambda b: first_send.at[b], lambda me: first_mid.at[me])
     first_freq = over_freq(1, lambda f: first_mid.at[:, f], lambda me: data_first_ref.at[me])
     second_freq = over_freq(2, lambda f: second_send.at[f], lambda me: second_mid.at[me])
@@ -209,9 +237,9 @@
     for m in range(4):
         load_traces(m).start()
     load_table(1).start()
-    carry, upper, row_i = index_work(rcv_ref, src_ref, pick_ref, cell_send, spread_ref, count_ref, start_ref)
+    carry, upper, row_i = index_work(rcv_ref, src_ref, pick_ref, cell_send, count_ref, start_ref)
     pl.semaphore_wait(pltpu.get_barrier_semaphore(), 22)
-    cell_bin.start()
+    cell_freq.start()
     list_runs(carry, upper, row_i, list_ref, edge_ref)
 
     def transform(h):
@@ -237,25 +265,39 @@
                 spread_ref[pl.ds(half * 4 + blk, 256, stride=8), :] = rows[:, blk * DEV : (blk + 1) * DEV]
 
     transform(0)
-    cell_bin.wait_recv()
-    cell_freq.start()
+    cell_freq.wait_recv()
+    cell_pack[...] = cell_mid[...].reshape(DEV, DEV).astype(jnp.int16)
+    cell_x.start()
     sort_rows()
     for b in range(8):
         first_send[b] = spread_ref[b * 256 : (b + 1) * 256, :].reshape(16, 16, DEV).astype(BF16)
     first_bin.start()
     transform(1)
+    cell_x.wait_recv()
+    cell_core.start()
     sort_rows()
     for f in range(16):
         second_send[f] = spread_ref[f * 128 : (f + 1) * 128, :].reshape(8, 16, DEV).astype(BF16)
     second_freq.start()
     first_bin.wait_recv()
     first_freq.start()
+    cell_core.wait_recv()
+    for c in range(2):
+        for x in range(4):
+            at = (x * 2 + c) * DEV
+            code_wide[at : at + DEV, :] = cell_all[c, x].astype(F32)
+    stride = TR + 16
+    for blk in range(8):
+        code = code_wide[pl.ds(blk, DEV, stride=8), :].T.astype(I32)
+        cell_rows_ref[blk * DEV : (blk + 1) * DEV, :] = (code >> 6).astype(F32)
+        cell_rows_ref[stride + blk * DEV : stride + (blk + 1) * DEV, :] = (code & 63).astype(F32)
+    for digit in range(2):
+        cell_rows_ref[digit * stride + TR : (digit + 1) * stride, :] = jnp.zeros((16, DEV), F32)
     second_freq.wait_recv()
     second_bin.start()
-    cell_freq.wait_recv()
     first_freq.wait_recv()
     second_bin.wait_recv()
-    for part in (cell_bin, cell_freq, first_bin, first_freq, second_freq, second_bin):
+    for part in (cell_freq, cell_x, cell_core, first_bin, first_freq, second_freq, second_bin):
         part.wait_send()
 
 
@@ -266,13 +308,11 @@
     edge_ref,
     first_ref,
     second_ref,
-    code_ref,
+    cell_ref,
     dense_ref,
     first_wide,
     second_wide,
-    code_wide,
     rows_ref,
-    cell_ref,
     raw_ref,
 ):
     stride = TR + 16
@@ -281,21 +321,17 @@
         for f in range(16):
             at = (b * 16 + f) * 16
             first_wide[at : at + 16, :] = first_ref[f, b].astype(F32)
-            code_wide[at : at + 16, :] = code_ref[f, b].astype(F32)
     for blk in range(8):
         for part in range(2):
             pick = pl.ds(part * 8 + blk, DEV, stride=16)
             rows_ref[pl.ds(part * stride + blk * DEV, DEV), :] = first_wide[pick, :].T
             rows_ref[pl.ds((2 + part) * stride + blk * DEV, DEV), :] = second_wide[pick, :].T
-            cell_ref[pl.ds(part * stride + blk * DEV, DEV), :] = code_wide[pick, :].T
     pad = jnp.zeros((16, DEV), F32)
     for comp in range(4):
         rows_ref[pl.ds(comp * stride + TR, 16), :] = pad
-    for digit in range(2):
-        cell_ref[pl.ds(digit * stride + TR, 16), :] = pad
-
-    sub16 = lax.broadcasted_iota(I32, (16, DEV), 0).astype(F32)
-    sub128 = lax.broadcasted_iota(I32, (DEV, DEV), 0).astype(F32).astype(BF16)
+
+    sub32 = lax.broadcasted_iota(I32, (32, DEV), 0).astype(F32)
+    sub64 = lax.broadcasted_iota(I32, (64, DEV), 0).astype(F32).astype(BF16)
     one, zero = jnp.ones((), BF16), jnp.zeros((), BF16)
 
     def lay_out(run, size):
@@ -304,16 +340,16 @@
         left, right = [], []
         for j in range(size):
             at = start + j
-            high = jnp.broadcast_to(cell_ref[pl.ds(at, 1), :], (16, DEV))
-            hit = jnp.where(j < count, high, -1.0) == sub16
+            high = jnp.broadcast_to(cell_ref[pl.ds(at, 1), :], (32, DEV))
+            hit = jnp.where(j < count, high, -1.0) == sub32
             parts = []
             for comp in range(4):
-                row = jnp.broadcast_to(rows_ref[pl.ds(comp * stride + at, 1), :], (16, DEV))
+                row = jnp.broadcast_to(rows_ref[pl.ds(comp * stride + at, 1), :], (32, DEV))
                 parts.append(jnp.where(hit, row, 0.0).astype(BF16))
             left.append(jnp.concatenate(parts, axis=0))
             low = jnp.broadcast_to(cell_ref[pl.ds(stride + at, 1), :], (16, DEV)).astype(BF16)
-            right.append(jnp.where(jnp.concatenate([low] * 8, axis=0) == sub128, one, zero))
-        raw_ref[run] = lax.dot_general(
+            right.append(jnp.where(jnp.concatenate([low] * 4, axis=0) == sub64, one, zero))
+        raw_ref[run, :, 0:64] = lax.dot_general(
             jnp.concatenate(left, axis=1),
             jnp.concatenate(right, axis=1),
             (((1,), (1,)), ((), ())),
@@ -321,7 +357,7 @@
         )
 
     begin = 0
-    for kind, (size, together) in enumerate(((4, 4), (8, 4), (16, 2))):
+    for kind, (size, together) in enumerate(((4, 8), (8, 8), (16, 4))):
         end = edge_ref[0, kind]
 
         def some_runs(step, _, begin=begin, end=end, size=size, together=together):
@@ -333,17 +369,20 @@
         begin = end
 
     top = lax.broadcasted_iota(I32, (8, DEV), 0) < 4
+    left_half = lax.broadcasted_iota(I32, (8, DEV), 1) < 64
 
     def four_runs(group, _):
         for comp in range(4):
             at = pl.ds(pl.multiple_of(comp * ORDER + group * 16, 16), 16)
-            for v in range(2):
-                sl = pl.ds(comp * 16 + 8 * v, 8)
-                a, b, c, d = [raw_ref[4 * group + u, sl, :] for u in range(4)]
-                first = [jnp.where(top, a, pltpu.roll(b, 4, 0)), jnp.where(top, c, pltpu.roll(d, 4, 0))]
-                last = [jnp.where(top, pltpu.roll(a, 4, 0), b), jnp.where(top, pltpu.roll(c, 4, 0), d)]
-                dense_ref[at, pl.ds(2 * v * DEV, DEV)] = jnp.concatenate(first, axis=0).astype(BF16)
-                dense_ref[at, pl.ds((2 * v + 1) * DEV, DEV)] = jnp.concatenate(last, axis=0).astype(BF16)
+            for tile in range(4):
+                sl = pl.ds(comp * 32 + 8 * tile, 8)
+                merged = []
+                for pair in range(2):
+                    even = raw_ref[4 * group + 2 * pair, sl, :]
+                    odd = raw_ref[4 * group + 2 * pair + 1, sl, :]
+                    right = pltpu.roll(pltpu.roll(jnp.where(top, odd, even), 4, 0), 64, 1)
+                    merged.append(jnp.where(left_half, jnp.where(top, even, odd), right))
+                dense_ref[at, pl.ds(tile * DEV, DEV)] = jnp.concatenate(merged, axis=0).astype(BF16)
         return 0
 
     lax.fori_loop(0, DEV // 4, four_runs, 0, unroll=2)
@@ -401,11 +440,11 @@
     first, second, cells, count, start, listed, edge = pl.pallas_call(
         spectrum_kernel,
         in_specs=[vmem, vmem, anywhere, anywhere, anywhere],
-        out_specs=(anywhere, anywhere, anywhere, vmem, vmem, vmem, vmem),
+        out_specs=(anywhere, anywhere, vmem, vmem, vmem, vmem, vmem),
         out_shape=(
             shape((16, 8, 16, DEV), BF16),
             shape((8, 16, 16, DEV), BF16),
-            shape((16, 8, 16, DEV), BF16),
+            shape((2 * (TR + 16), DEV), F32),
             small,
             small,
             small,
@@ -417,8 +456,11 @@
             pltpu.VMEM((TR, TR), BF16),
             pltpu.VMEM((TR, 256), BF16),
             pltpu.VMEM((2048, DEV), F32),
-            pltpu.VMEM((16, DEV), BF16),
-            pltpu.VMEM((8, 16, DEV), BF16),
+            pltpu.VMEM((8, DEV), I32),
+            pltpu.VMEM((16, 8, DEV), I32),
+            pltpu.VMEM((DEV, DEV), jnp.int16),
+            pltpu.VMEM((2, 4, DEV, DEV), jnp.int16),
+            pltpu.VMEM((TR, DEV), F32),
             outgoing,
             outgoing,
             middle,
@@ -428,6 +470,8 @@
             dma((3, 8)),
             dma((3, 16)),
             dma((3, 16)),
+            dma((2,)),
+            dma((2,)),
         ],
         compiler_params=pltpu.CompilerParams(vmem_limit_bytes=LIMIT, collective_id=1, has_side_effects=True),
         cost_estimate=pl.CostEstimate(flops=5 * 10**9, bytes_accessed=9 * 10**6, transcendentals=0),
@@ -441,10 +485,8 @@
         scratch_shapes=[
             pltpu.VMEM((2048, DEV), F32),
             pltpu.VMEM((2048, DEV), F32),
-            pltpu.VMEM((2048, DEV), F32),
             pltpu.VMEM((4 * (TR + 16), DEV), F32),
-            pltpu.VMEM((2 * (TR + 16), DEV), F32),
-            pltpu.VMEM((DEV, 64, DEV), F32),
+            pltpu.VMEM((DEV, DEV, DEV), F32),
         ],
         compiler_params=params,
         name="layout",

time: 92.7 us -> 89.4 us (0.964)
  Pallas kernels: 89.4 us -> 86 us
    pallas_call x1, Pallas kernels: 21.1 us -> 17.6 us  [local(): pl.pallas_call(layout_kernel, in_specs=[smem, smem, smem, smem, vmem, vme...]
where the time goes in v4:
time: 89.4 us; the launch traced here: 89.2 us
  Pallas kernels  86 us (96%)
  local copies, waits for them, and re-layouts  3.13 us (4%)
    pallas_call x1, Pallas kernels, local(): pl.pallas_call(spectrum_kernel, in_specs=[vmem, vmem, anywhere, anywhere,...  39.9 us
    pallas_call x1, Pallas kernels, local(): pl.pallas_call(product_kernel, in_specs=[smem, vmem], out_specs=anywhere,...  28.5 us
    pallas_call x1, Pallas kernels, local(): pl.pallas_call(layout_kernel, in_specs=[smem, smem, smem, smem, vmem, vme...  17.6 us
    unnamed x1, local copies, waits for them, and re-layouts  3.13 us

profile of v4, /device:TPU:1, one launch (start us, length us, event | category | flops | bytes accessed | tf_op | source)
XLA Modules:
  0.0 89.2 jit_solution(9155701014659402215)
XLA Ops:
  0.0 39.9 %spectrum.1 = (bf16[16,8,16,128]{3,2,1,0:T(8,128)(2,1)}, bf16[8,16,16,128]{3,2,1,0:T(8,128)(2,1)}, f32[2080,128]{1,0:T(8,128)}, s32[8,128]{1,0:T(8,128)}, s32[8,...) custom-call(s32[8,128]{1,0:T(8,128)} %bitcast.2, s32[8,128]{1,0:T(8,128)} %bitcast.3, ...), custom_call_target="tpu_custom_call" | custom-call | flops 5000000000 | bytes 9000000 | tf_op jit(solution)/shard_map/spectrum/pallas_call | solution.py:440
  39.9 17.6 %layout.1.dense_ref = bf16[2048,512]{1,0:T(8,128)(2,1)} custom-call(s32[8,128]{1,0:T(8,128)} %get-tuple-element.12.count_ref, s32[8,128]{1,0:T(8,128)} %get-tuple-element.13.start_ref, s32[8,128]{1,0:T(8,128)} %get-tuple-element.14.list_ref, s32[8,128]{1,0:T(8,128)} %get-tuple-element.15.edge_ref, bf16[16,8,16,128]{3,2,1,0:T(8,128)(2,1)} %get-tuple-element.16.first_ref, ...), custom_call_target="tpu_custom_call" | custom-call | tf_op jit(solution)/shard_map/layout/pallas_call | solution.py:480
  57.5 28.5 %product.1 = bf16[2,16,64,512]{3,2,1,0:T(8,128)(2,1)} custom-call(f32[2,16]{1,0:T(2,128)} %filt_ref.1, bf16[2048,512]{1,0:T(8,128)(2,1)} %layout.1.dense_ref), custom_call_target="tpu_custom_call" | custom-call | tf_op jit(solution)/shard_map/product/pallas_call | solution.py:494
  86.0 3.1 %copy.8 = bf16[2,16,64,512]{3,2,1,0:T(8,128)(2,1)} copy(bf16[2,16,64,512]{3,2,1,0:T(8,128)(2,1)} %product.1) | data formatting | bytes 4194304

commit v5 on v4

--- a/solution.py
+++ b/solution.py
@@ -42,14 +42,14 @@
     lower = (col_i < row_i).astype(BF16)
     upper = (row_i < col_i).astype(BF16)
     same = row_i == col_i
-    rcv_cols, src_cols = [], []
+    rcv = rcv_ref[...]
+    src = src_ref[...]
+    run = (rcv >> 2).astype(F32)
+    columns = []
     for blk in range(TR // DEV):
-        for cols, ref in ((rcv_cols, rcv_ref), (src_cols, src_ref)):
-            spread = jnp.where(same, jnp.broadcast_to(ref[blk : blk + 1, :], (DEV, DEV)), 0)
-            cols.append(jnp.sum(spread.astype(F32), axis=1, keepdims=True).astype(I32))
-    rcv = jnp.concatenate(rcv_cols, axis=0)
-    src = jnp.concatenate(src_cols, axis=0)
-    member = (rcv // 4 == lane).astype(F32)
+        spread = jnp.where(same, jnp.broadcast_to(run[blk : blk + 1, :], (DEV, DEV)), 0.0)
+        columns.append(jnp.sum(spread, axis=1, keepdims=True))
+    member = (jnp.concatenate(columns, axis=0).astype(I32) == lane).astype(F32)
     carry = jnp.zeros((1, DEV), F32)
     ranks = []
     for blk in range(TR // DEV):
@@ -62,16 +62,16 @@
     place = jnp.sum(member * (rank_all + start[0:1]), axis=1, keepdims=True).astype(I32)
     count_ref[...] = counts8.astype(I32)
     start_ref[...] = start.astype(I32)
-    half = (src // 64 + rcv // 4) % 2
-    high = ((src // 128) * 8 + half * 4 + rcv % 4).astype(F32)
-    low = (src % 64).astype(F32)
-    digit = lax.broadcasted_iota(I32, (TR, DEV), 1)
-    digits = jnp.where(digit == 0, high, jnp.where(digit == 1, low, 0.0)).astype(BF16)
     pick_ref[...] = (place == lax.broadcasted_iota(I32, (TR, TR), 1)).astype(F32).astype(BF16)
-    both = lax.dot_general(digits, pick_ref[...], (((0,), (0,)), ((), ())), preferred_element_type=F32)
+    half = ((src >> 6) + (rcv >> 2)) & 1
+    high = ((src >> 7) * 8 + half * 4 + (rcv & 3)).astype(F32)
+    low = (src & 63).astype(F32)
+    flat = [jnp.concatenate([v[blk : blk + 1, :] for blk in range(TR // DEV)], axis=1) for v in (high, low)]
+    digits = jnp.concatenate([jnp.broadcast_to(v, (8, TR)) for v in flat], axis=0).astype(BF16)
+    both = jnp.dot(digits, pick_ref[...], preferred_element_type=F32)
     for blk in range(TR // DEV):
         cols = slice(blk * DEV, (blk + 1) * DEV)
-        cell_ref[blk : blk + 1, :] = (both[0:1, cols] * 64.0 + both[1:2, cols]).astype(I32)
+        cell_ref[blk : blk + 1, :] = (both[0:1, cols] * 64.0 + both[8:9, cols]).astype(I32)
     return carry, upper, row_i
 
 
@@ -273,14 +273,14 @@
         first_send[b] = spread_ref[b * 256 : (b + 1) * 256, :].reshape(16, 16, DEV).astype(BF16)
     first_bin.start()
     transform(1)
-    cell_x.wait_recv()
-    cell_core.start()
     sort_rows()
     for f in range(16):
         second_send[f] = spread_ref[f * 128 : (f + 1) * 128, :].reshape(8, 16, DEV).astype(BF16)
     second_freq.start()
     first_bin.wait_recv()
     first_freq.start()
+    cell_x.wait_recv()
+    cell_core.start()
     cell_core.wait_recv()
     for c in range(2):
         for x in range(4):
@@ -330,7 +330,7 @@
     for comp in range(4):
         rows_ref[pl.ds(comp * stride + TR, 16), :] = pad
 
-    sub32 = lax.broadcasted_iota(I32, (32, DEV), 0).astype(F32)
+    sub32 = lax.broadcasted_iota(I32, (32, DEV), 0).astype(F32).astype(BF16)
     sub64 = lax.broadcasted_iota(I32, (64, DEV), 0).astype(F32).astype(BF16)
     one, zero = jnp.ones((), BF16), jnp.zeros((), BF16)
 
@@ -340,12 +340,13 @@
         left, right = [], []
         for j in range(size):
             at = start + j
-            high = jnp.broadcast_to(cell_ref[pl.ds(at, 1), :], (32, DEV))
-            hit = jnp.where(j < count, high, -1.0) == sub32
+            high = jnp.broadcast_to(cell_ref[pl.ds(at, 1), :], (16, DEV))
+            high = jnp.where(j < count, high, -1.0).astype(BF16)
+            hit = jnp.concatenate([high] * 2, axis=0) == sub32
             parts = []
             for comp in range(4):
-                row = jnp.broadcast_to(rows_ref[pl.ds(comp * stride + at, 1), :], (32, DEV))
-                parts.append(jnp.where(hit, row, 0.0).astype(BF16))
+                row = jnp.broadcast_to(rows_ref[pl.ds(comp * stride + at, 1), :], (16, DEV)).astype(BF16)
+                parts.append(jnp.where(hit, jnp.concatenate([row] * 2, axis=0), zero))
             left.append(jnp.concatenate(parts, axis=0))
             low = jnp.broadcast_to(cell_ref[pl.ds(stride + at, 1), :], (16, DEV)).astype(BF16)
             right.append(jnp.where(jnp.concatenate([low] * 4, axis=0) == sub64, one, zero))
@@ -357,7 +358,7 @@
         )
 
     begin = 0
-    for kind, (size, together) in enumerate(((4, 8), (8, 8), (16, 4))):
+    for kind, (size, together) in enumerate(((4, 32), (8, 32), (16, 16))):
         end = edge_ref[0, kind]
 
         def some_runs(step, _, begin=begin, end=end, size=size, together=together):
@@ -425,6 +426,18 @@
     for move in moves:
         move.wait_recv()
         move.wait_send()
+
+
+def hand_over(rows_ref, out_ref, hold_ref, sem):
+    loads = [pltpu.make_async_copy(rows_ref.at[:, i], hold_ref.at[:, i], sem.at[0, i]) for i in range(16)]
+    stores = [pltpu.make_async_copy(hold_ref.at[:, i], out_ref.at[:, i], sem.at[1, i]) for i in range(16)]
+    for load in loads:
+        load.start()
+    for load, store in zip(loads, stores):
+        load.wait()
+        store.start()
+    for store in stores:
+        store.wait()
 
 
 def local(traces, rcv_index, src_index, wave_filter):
@@ -491,7 +504,7 @@
         compiler_params=params,
         name="layout",
     )(count, start, listed, edge, first, second, cells)
-    return pl.pallas_call(
+    rows = pl.pallas_call(
         product_kernel,
         in_specs=[smem, vmem],
         out_specs=anywhere,
@@ -500,6 +513,15 @@
         compiler_params=pltpu.CompilerParams(vmem_limit_bytes=LIMIT, collective_id=2, has_side_effects=True),
         name="product",
     )(wave_filter, dense)
+    return pl.pallas_call(
+        hand_over,
+        in_specs=[anywhere],
+        out_specs=anywhere,
+        out_shape=shape((2, 16, 64, ORDER), BF16),
+        scratch_shapes=[pltpu.VMEM((2, 16, 64, ORDER), BF16), dma((2, 16))],
+        compiler_params=params,
+        name="hand_over",
+    )(rows)
 
 
 def solution(mesh):

time: 89.4 us -> 82.5 us (0.923)
  Pallas kernels: 86 us -> 82.3 us
  local copies, waits for them, and re-layouts: 3.13 us -> 0 us
    pallas_call x1, Pallas kernels: 39.9 us -> 35.6 us  [local(): pl.pallas_call(spectrum_kernel, in_specs=[vmem, vmem, anywhere, anywhere,...]
    unnamed x1 -> x0, local copies, waits for them, and re-layouts: 3.13 us -> none
    pallas_call x0 -> x1, Pallas kernels: none -> 2.57 us  [local(): pl.pallas_call(hand_over, in_specs=[anywhere], out_specs=anywhere, out_sh...]
    pallas_call x1, Pallas kernels: 17.6 us -> 15.2 us  [local(): pl.pallas_call(layout_kernel, in_specs=[smem, smem, smem, smem, vmem, vme...]
where the time goes in v5:
time: 82.5 us; the launch traced here: 82.3 us
  Pallas kernels  82.3 us (100%)
    pallas_call x1, Pallas kernels, local(): pl.pallas_call(spectrum_kernel, in_specs=[vmem, vmem, anywhere, anywhere,...  35.6 us
    pallas_call x1, Pallas kernels, local(): pl.pallas_call(product_kernel, in_specs=[smem, vmem], out_specs=anywhere,...  28.9 us
    pallas_call x1, Pallas kernels, local(): pl.pallas_call(layout_kernel, in_specs=[smem, smem, smem, smem, vmem, vme...  15.2 us
    pallas_call x1, Pallas kernels, local(): pl.pallas_call(hand_over, in_specs=[anywhere], out_specs=anywhere, out_sh...  2.57 us

profile of v5, /device:TPU:1, one launch (start us, length us, event | category | flops | bytes accessed | tf_op | source)
XLA Modules:
  0.0 82.3 jit_solution(15592512947604137910)
XLA Ops:
  0.0 35.6 %spectrum.1 = (bf16[16,8,16,128]{3,2,1,0:T(8,128)(2,1)}, bf16[8,16,16,128]{3,2,1,0:T(8,128)(2,1)}, f32[2080,128]{1,0:T(8,128)}, s32[8,128]{1,0:T(8,128)}, s32[8,...) custom-call(s32[8,128]{1,0:T(8,128)} %bitcast.2, s32[8,128]{1,0:T(8,128)} %bitcast.3, ...), custom_call_target="tpu_custom_call" | custom-call | flops 5000000000 | bytes 9000000 | tf_op jit(solution)/shard_map/spectrum/pallas_call | solution.py:453
  35.6 15.2 %layout.1.dense_ref = bf16[2048,512]{1,0:T(8,128)(2,1)} custom-call(s32[8,128]{1,0:T(8,128)} %get-tuple-element.12.count_ref, s32[8,128]{1,0:T(8,128)} %get-tuple-element.13.start_ref, s32[8,128]{1,0:T(8,128)} %get-tuple-element.14.list_ref, s32[8,128]{1,0:T(8,128)} %get-tuple-element.15.edge_ref, bf16[16,8,16,128]{3,2,1,0:T(8,128)(2,1)} %get-tuple-element.16.first_ref, ...), custom_call_target="tpu_custom_call" | custom-call | tf_op jit(solution)/shard_map/layout/pallas_call | solution.py:493
  50.8 28.9 %product.1.rows_ref = bf16[2,16,64,512]{3,2,1,0:T(8,128)(2,1)} custom-call(f32[2,16]{1,0:T(2,128)} %filt_ref.1, bf16[2048,512]{1,0:T(8,128)(2,1)} %layout.1.dense_ref), custom_call_target="tpu_custom_call" | custom-call | tf_op jit(solution)/shard_map/product/pallas_call | solution.py:507
  79.7 2.6 %hand_over.1 = bf16[2,16,64,512]{3,2,1,0:T(8,128)(2,1)} custom-call(bf16[2,16,64,512]{3,2,1,0:T(8,128)(2,1)} %product.1.rows_ref), custom_call_target="tpu_custom_call" | custom-call | tf_op jit(solution)/shard_map/hand_over/pallas_call | solution.py:516

commit v6 on v5

--- a/solution.py
+++ b/solution.py
@@ -240,7 +240,6 @@
     carry, upper, row_i = index_work(rcv_ref, src_ref, pick_ref, cell_send, count_ref, start_ref)
     pl.semaphore_wait(pltpu.get_barrier_semaphore(), 22)
     cell_freq.start()
-    list_runs(carry, upper, row_i, list_ref, edge_ref)
 
     def transform(h):
         load_table(h).wait()
@@ -265,18 +264,19 @@
                 spread_ref[pl.ds(half * 4 + blk, 256, stride=8), :] = rows[:, blk * DEV : (blk + 1) * DEV]
 
     transform(0)
+    sort_rows()
+    for b in range(8):
+        first_send[b] = spread_ref[b * 256 : (b + 1) * 256, :].reshape(16, 16, DEV).astype(BF16)
     cell_freq.wait_recv()
     cell_pack[...] = cell_mid[...].reshape(DEV, DEV).astype(jnp.int16)
     cell_x.start()
-    sort_rows()
-    for b in range(8):
-        first_send[b] = spread_ref[b * 256 : (b + 1) * 256, :].reshape(16, 16, DEV).astype(BF16)
     first_bin.start()
     transform(1)
     sort_rows()
     for f in range(16):
         second_send[f] = spread_ref[f * 128 : (f + 1) * 128, :].reshape(8, 16, DEV).astype(BF16)
     second_freq.start()
+    list_runs(carry, upper, row_i, list_ref, edge_ref)
     first_bin.wait_recv()
     first_freq.start()
     cell_x.wait_recv()
@@ -389,7 +389,12 @@
     lax.fori_loop(0, DEV // 4, four_runs, 0, unroll=2)
 
 
-def product_kernel(filt_ref, dense_ref, out_ref, block_ref, send, recv):
+def product_kernel(filt_ref, dense_ref, out_ref, hold_ref, block_ref, load_sem, send, recv):
+    loads = []
+    for i in range(2):
+        part = pl.ds(2 * i * ORDER, 2 * ORDER)
+        loads.append(pltpu.make_async_copy(dense_ref.at[part], hold_ref.at[part], load_sem.at[i]))
+        loads[-1].start()
     mine = lax.axis_index("bin") * 2
     amplitude = 1.0 / math.sqrt(ORDER)
     greet((("bin", 8),))
@@ -405,8 +410,9 @@
         for i in range(2)
     ]
     for i in range(2):
-        real = dense_ref[pl.ds(2 * i * ORDER, ORDER), :]
-        imag = dense_ref[pl.ds((2 * i + 1) * ORDER, ORDER), :]
+        loads[i].wait()
+        real = hold_ref[pl.ds(2 * i * ORDER, ORDER), :]
+        imag = hold_ref[pl.ds((2 * i + 1) * ORDER, ORDER), :]
         fr = filt_ref[0, mine + i]
         fi = filt_ref[1, mine + i]
         for t in range(2):
@@ -506,10 +512,16 @@
     )(count, start, listed, edge, first, second, cells)
     rows = pl.pallas_call(
         product_kernel,
-        in_specs=[smem, vmem],
+        in_specs=[smem, anywhere],
         out_specs=anywhere,
         out_shape=shape((2, 16, 64, ORDER), BF16),
-        scratch_shapes=[pltpu.VMEM((8, 2, 2, 64, ORDER), BF16), dma((2, 8)), dma((2, 8))],
+        scratch_shapes=[
+            pltpu.VMEM((4 * ORDER, ORDER), BF16),
+            pltpu.VMEM((8, 2, 2, 64, ORDER), BF16),
+            dma((2,)),
+            dma((2, 8)),
+            dma((2, 8)),
+        ],
         compiler_params=pltpu.CompilerParams(vmem_limit_bytes=LIMIT, collective_id=2, has_side_effects=True),
         name="product",
     )(wave_filter, dense)

time: 82.5 us -> 81.8 us (level)
    pallas_call x1, Pallas kernels: 35.6 us -> 34.1 us  [local(): pl.pallas_call(spectrum_kernel, in_specs=[vmem, vmem, anywhere, anywhere,...]
where the time goes in v6:
time: 81.8 us; the launch traced here: 81.6 us
  Pallas kernels  81.6 us (100%)
    pallas_call x1, Pallas kernels, local(): pl.pallas_call(spectrum_kernel, in_specs=[vmem, vmem, anywhere, anywhere,...  34.1 us
    pallas_call x1, Pallas kernels, local(): pl.pallas_call(product_kernel, in_specs=[smem, anywhere], out_specs=anywh...  29.7 us
    pallas_call x1, Pallas kernels, local(): pl.pallas_call(layout_kernel, in_specs=[smem, smem, smem, smem, vmem, vme...  15.2 us
    pallas_call x1, Pallas kernels, local(): pl.pallas_call(hand_over, in_specs=[anywhere], out_specs=anywhere, out_sh...  2.57 us

profile of v6, /device:TPU:1, one launch (start us, length us, event | category | flops | bytes accessed | tf_op | source)
XLA Modules:
  0.0 81.6 jit_solution(1561939923076534751)
XLA Ops:
  0.0 34.1 %spectrum.1 = (bf16[16,8,16,128]{3,2,1,0:T(8,128)(2,1)}, bf16[8,16,16,128]{3,2,1,0:T(8,128)(2,1)}, f32[2080,128]{1,0:T(8,128)}, s32[8,128]{1,0:T(8,128)}, s32[8,...) custom-call(s32[8,128]{1,0:T(8,128)} %bitcast.2, s32[8,128]{1,0:T(8,128)} %bitcast.3, ...), custom_call_target="tpu_custom_call" | custom-call | flops 5000000000 | bytes 9000000 | tf_op jit(solution)/shard_map/spectrum/pallas_call | solution.py:459
  34.1 15.2 %layout.1.dense_ref = bf16[2048,512]{1,0:T(8,128)(2,1)} custom-call(s32[8,128]{1,0:T(8,128)} %get-tuple-element.12.count_ref, s32[8,128]{1,0:T(8,128)} %get-tuple-element.13.start_ref, s32[8,128]{1,0:T(8,128)} %get-tuple-element.14.list_ref, s32[8,128]{1,0:T(8,128)} %get-tuple-element.15.edge_ref, bf16[16,8,16,128]{3,2,1,0:T(8,128)(2,1)} %get-tuple-element.16.first_ref, ...), custom_call_target="tpu_custom_call" | custom-call | tf_op jit(solution)/shard_map/layout/pallas_call | solution.py:499
  49.3 29.7 %product.1.rows_ref = bf16[2,16,64,512]{3,2,1,0:T(8,128)(2,1)} custom-call(f32[2,16]{1,0:T(2,128)} %filt_ref.1, bf16[2048,512]{1,0:T(8,128)(2,1)} %layout.1.dense_ref), custom_call_target="tpu_custom_call" | custom-call | tf_op jit(solution)/shard_map/product/pallas_call | solution.py:513
  79.0 2.6 %hand_over.1 = bf16[2,16,64,512]{3,2,1,0:T(8,128)(2,1)} custom-call(bf16[2,16,64,512]{3,2,1,0:T(8,128)(2,1)} %product.1.rows_ref), custom_call_target="tpu_custom_call" | custom-call | tf_op jit(solution)/shard_map/hand_over/pallas_call | solution.py:528

commit v7 on v6

--- a/solution.py
+++ b/solution.py
@@ -143,6 +143,13 @@
         lax.fori_loop(1, self.size, step, 0)
 
 
+def far_first(k):
+    me = lax.axis_index("bin")
+    turn = (k - 1) // 2
+    away = jnp.where(turn == 0, 2, jnp.where(turn == 1, 1, jnp.where(turn == 2, 3, 0)))
+    return lax.rem(me // 2 + away, 4) * 2 + lax.rem(me + k, 2)
+
+
 def greet(axes):
     barrier = pltpu.get_barrier_semaphore()
     for axis, size in axes:
@@ -406,6 +413,7 @@
             lambda me, i=i: out_ref.at[:, me * 2 + i],
             send.at[i],
             recv.at[i],
+            peers=far_first,
         )
         for i in range(2)
     ]

time: 81.8 us -> 80.3 us (0.982)
  Pallas kernels: 81.6 us -> 80.1 us
    pallas_call x1, Pallas kernels: 29.7 us -> 28.2 us  [local(): pl.pallas_call(product_kernel, in_specs=[smem, anywhere], out_specs=anywh...]
where the time goes in v7:
time: 80.3 us; the launch traced here: 80.1 us
  Pallas kernels  80.1 us (100%)
    pallas_call x1, Pallas kernels, local(): pl.pallas_call(spectrum_kernel, in_specs=[vmem, vmem, anywhere, anywhere,...  34.1 us
    pallas_call x1, Pallas kernels, local(): pl.pallas_call(product_kernel, in_specs=[smem, anywhere], out_specs=anywh...  28.2 us
    pallas_call x1, Pallas kernels, local(): pl.pallas_call(layout_kernel, in_specs=[smem, smem, smem, smem, vmem, vme...  15.2 us
    pallas_call x1, Pallas kernels, local(): pl.pallas_call(hand_over, in_specs=[anywhere], out_specs=anywhere, out_sh...  2.57 us

profile of v7, /device:TPU:1, one launch (start us, length us, event | category | flops | bytes accessed | tf_op | source)
XLA Modules:
  0.0 80.1 jit_solution(16888846495701715017)
XLA Ops:
  0.0 34.1 %spectrum.1 = (bf16[16,8,16,128]{3,2,1,0:T(8,128)(2,1)}, bf16[8,16,16,128]{3,2,1,0:T(8,128)(2,1)}, f32[2080,128]{1,0:T(8,128)}, s32[8,128]{1,0:T(8,128)}, s32[8,...) custom-call(s32[8,128]{1,0:T(8,128)} %bitcast.2, s32[8,128]{1,0:T(8,128)} %bitcast.3, ...), custom_call_target="tpu_custom_call" | custom-call | flops 5000000000 | bytes 9000000 | tf_op jit(solution)/shard_map/spectrum/pallas_call | solution.py:467
  34.1 15.2 %layout.1.dense_ref = bf16[2048,512]{1,0:T(8,128)(2,1)} custom-call(s32[8,128]{1,0:T(8,128)} %get-tuple-element.12.count_ref, s32[8,128]{1,0:T(8,128)} %get-tuple-element.13.start_ref, s32[8,128]{1,0:T(8,128)} %get-tuple-element.14.list_ref, s32[8,128]{1,0:T(8,128)} %get-tuple-element.15.edge_ref, bf16[16,8,16,128]{3,2,1,0:T(8,128)(2,1)} %get-tuple-element.16.first_ref, ...), custom_call_target="tpu_custom_call" | custom-call | tf_op jit(solution)/shard_map/layout/pallas_call | solution.py:507
  49.3 28.2 %product.1.rows_ref = bf16[2,16,64,512]{3,2,1,0:T(8,128)(2,1)} custom-call(f32[2,16]{1,0:T(2,128)} %filt_ref.1, bf16[2048,512]{1,0:T(8,128)(2,1)} %layout.1.dense_ref), custom_call_target="tpu_custom_call" | custom-call | tf_op jit(solution)/shard_map/product/pallas_call | solution.py:521
  77.5 2.6 %hand_over.1 = bf16[2,16,64,512]{3,2,1,0:T(8,128)(2,1)} custom-call(bf16[2,16,64,512]{3,2,1,0:T(8,128)(2,1)} %product.1.rows_ref), custom_call_target="tpu_custom_call" | custom-call | tf_op jit(solution)/shard_map/hand_over/pallas_call | solution.py:536

commit v8 on v7

--- a/solution.py
+++ b/solution.py
@@ -122,7 +122,11 @@
             self.copy(k).start()
             return 0
 
-        lax.fori_loop(1, self.size, step, 0)
+        if self.axis == "freq":
+            for k in FAR_FIRST:
+                step(k, 0)
+        else:
+            lax.fori_loop(1, self.size, step, 0)
         if self.keep:
             self.own().start()
 
@@ -148,6 +152,14 @@
     turn = (k - 1) // 2
     away = jnp.where(turn == 0, 2, jnp.where(turn == 1, 1, jnp.where(turn == 2, 3, 0)))
     return lax.rem(me // 2 + away, 4) * 2 + lax.rem(me + k, 2)
+
+
+def turned(k):
+    me = lax.axis_index("freq")
+    return lax.rem(me // 4 + k // 4, 4) * 4 + lax.rem(me + lax.rem(k, 4), 4)
+
+
+FAR_FIRST = (10, 9, 11, 6, 14, 8, 2, 5, 7, 13, 15, 1, 3, 4, 12)
 
 
 def greet(axes):
@@ -203,7 +215,7 @@
         return Exchange("bin", 8, source, target, bin_send.at[slot], bin_recv.at[slot])
 
     def over_freq(slot, source, target):
-        return Exchange("freq", 16, source, target, freq_send.at[slot], freq_recv.at[slot])
+        return Exchange("freq", 16, source, target, freq_send.at[slot], freq_recv.at[slot], peers=turned)
 
     bin_me = lax.axis_index("bin")
     core, x_me = lax.rem(bin_me, 2), bin_me // 2

time: 80.3 us -> 84.3 us (1.050)
  Pallas kernels: 80.1 us -> 84 us
    pallas_call x1, Pallas kernels: 34.1 us -> 38.9 us  [local(): pl.pallas_call(spectrum_kernel, in_specs=[vmem, vmem, anywhere, anywhere,...]
    pallas_call x1, Pallas kernels: 28.2 us -> 27.3 us  [local(): pl.pallas_call(product_kernel, in_specs=[smem, anywhere], out_specs=anywh...]
where the time goes in v8:
time: 84.3 us; the launch traced here: 84.1 us
  Pallas kernels  84 us (100%)
    pallas_call x1, Pallas kernels, local(): pl.pallas_call(spectrum_kernel, in_specs=[vmem, vmem, anywhere, anywhere,...  38.9 us
    pallas_call x1, Pallas kernels, local(): pl.pallas_call(product_kernel, in_specs=[smem, anywhere], out_specs=anywh...  27.3 us
    pallas_call x1, Pallas kernels, local(): pl.pallas_call(layout_kernel, in_specs=[smem, smem, smem, smem, vmem, vme...  15.2 us
    pallas_call x1, Pallas kernels, local(): pl.pallas_call(hand_over, in_specs=[anywhere], out_specs=anywhere, out_sh...  2.57 us

profile of v8, /device:TPU:1, one launch (start us, length us, event | category | flops | bytes accessed | tf_op | source)
XLA Modules:
  0.0 84.1 jit_solution(12979467017349465899)
XLA Ops:
  0.0 38.9 %spectrum.1 = (bf16[16,8,16,128]{3,2,1,0:T(8,128)(2,1)}, bf16[8,16,16,128]{3,2,1,0:T(8,128)(2,1)}, f32[2080,128]{1,0:T(8,128)}, s32[8,128]{1,0:T(8,128)}, s32[8,...) custom-call(s32[8,128]{1,0:T(8,128)} %bitcast.2, s32[8,128]{1,0:T(8,128)} %bitcast.3, ...), custom_call_target="tpu_custom_call" | custom-call | flops 5000000000 | bytes 9000000 | tf_op jit(solution)/shard_map/spectrum/pallas_call | solution.py:479
  38.9 15.2 %layout.1.dense_ref = bf16[2048,512]{1,0:T(8,128)(2,1)} custom-call(s32[8,128]{1,0:T(8,128)} %get-tuple-element.12.count_ref, s32[8,128]{1,0:T(8,128)} %get-tuple-element.13.start_ref, s32[8,128]{1,0:T(8,128)} %get-tuple-element.14.list_ref, s32[8,128]{1,0:T(8,128)} %get-tuple-element.15.edge_ref, bf16[16,8,16,128]{3,2,1,0:T(8,128)(2,1)} %get-tuple-element.16.first_ref, ...), custom_call_target="tpu_custom_call" | custom-call | tf_op jit(solution)/shard_map/layout/pallas_call | solution.py:519
  54.2 27.3 %product.1.rows_ref = bf16[2,16,64,512]{3,2,1,0:T(8,128)(2,1)} custom-call(f32[2,16]{1,0:T(2,128)} %filt_ref.1, bf16[2048,512]{1,0:T(8,128)(2,1)} %layout.1.dense_ref), custom_call_target="tpu_custom_call" | custom-call | tf_op jit(solution)/shard_map/product/pallas_call | solution.py:533
  81.5 2.6 %hand_over.1 = bf16[2,16,64,512]{3,2,1,0:T(8,128)(2,1)} custom-call(bf16[2,16,64,512]{3,2,1,0:T(8,128)(2,1)} %product.1.rows_ref), custom_call_target="tpu_custom_call" | custom-call | tf_op jit(solution)/shard_map/hand_over/pallas_call | solution.py:548
